TPU v7x, 32 devices: a whole 2x2x4 slice. The times are simulated.
32 devices in a mesh: groups: 2 (over x), dap: 16 (over z, y, core).
Axes of the slice: x: 2, y: 2, z: 4, core: 2. Of those that a mesh axis runs over, the one named last changes fastest.
Arguments:
- pair: bfloat16 [640, 320, 128], P(('groups', 'dap')), parts along dimension 0, may hold values from -6 to 6
- d_out: bfloat16 [640, 320, 128], P(('groups', 'dap')), parts along dimension 0, may hold values from -6 to 6
- residue_mask: int32 [640], P('groups'), parts along dimension 0, may hold values from 0 to 1, as said below
- w_in: bfloat16 [128, 512], replicated, may hold values from -0.5 to 0.5
- w_gate: bfloat16 [128, 128], replicated, may hold values from -0.5 to 0.5
- w_out: bfloat16 [128, 128], replicated, may hold values from -0.5 to 0.5
Outputs:
- update: bfloat16 [640, 320, 128], P(('groups', 'dap')), parts along dimension 0
- d_pair: bfloat16 [640, 320, 128], P(('groups', 'dap')), parts along dimension 0
- d_w_in: float32 [256, 512], P('groups'), parts along dimension 0
- d_w_gate: float32 [256, 128], P('groups'), parts along dimension 0
- d_w_out: float32 [256, 128], P('groups'), parts along dimension 0
There are 2 independent parts, one for each index of `groups`. A program takes and returns all parts, laid end to end along the dimension named above; an argument that names none is the same for every part. Nothing has to cross between parts.
Inputs may be any that keep to these rules, and one draw needn't show every extreme that they name: `residue_mask`: 1 for the first residues of a crop and 0 after them; at least 160 ones.
All inputs are finite; a program needn't handle non-finite values.
Results may differ from a plain program's by a relative error of at most 0.0089.
Values may be sent and summed in bfloat16 or wider, within the bound.
A program may use at most 192 MiB of HBM per device.

v0:
```python
import jax
import jax.numpy as jnp
from jax import lax
from jax.sharding import PartitionSpec as P


def norm_axis(values, axis):
    center = values - jnp.mean(values, axis=axis, keepdims=True)
    inverse = lax.rsqrt(jnp.mean(center * center, axis=axis, keepdims=True) + 1e-05)
    return center * inverse


def norm_back(cotan, values, axis):
    center = values - jnp.mean(values, axis=axis, keepdims=True)
    inverse = lax.rsqrt(jnp.mean(center * center, axis=axis, keepdims=True) + 1e-05)
    normed = center * inverse
    shifted = cotan - jnp.mean(cotan, axis=axis, keepdims=True)
    return inverse * (shifted - normed * jnp.mean(cotan * normed, axis=axis, keepdims=True))


def project(normed, weight):
    return jnp.einsum("ric,ch->hri", normed, weight, preferred_element_type=jnp.float32)


def triangle(pieces):
    left_part, right_part = pieces
    return jnp.einsum(
        "qhki,qhkj->qhij", left_part, right_part, preferred_element_type=jnp.float32
    ).astype(jnp.bfloat16)


def shards(pair, d_out, residue_mask, w_in, w_gate, w_out):
    row_count = pair.shape[0]
    crop_len = pair.shape[1]
    hidden = w_out.shape[0]
    row_start = lax.axis_index("dap") * row_count
    mask_all = residue_mask.astype(jnp.float32)
    mask_rows = lax.dynamic_slice_in_dim(mask_all, row_start, row_count, 0)
    pmask = (mask_rows[:, None] * mask_all[None, :])[None]
    pair_f = pair.astype(jnp.float32)
    normed = norm_axis(pair_f, -1).astype(jnp.bfloat16)
    lin_a = project(normed, w_in[:, 0:hidden])
    gate_a = project(normed, w_in[:, hidden : 2 * hidden])
    lin_b = project(normed, w_in[:, 2 * hidden : 3 * hidden])
    gate_b = project(normed, w_in[:, 3 * hidden : 4 * hidden])
    sig_a = jax.nn.sigmoid(gate_a)
    sig_b = jax.nn.sigmoid(gate_b)
    left = (pmask * sig_a * lin_a).astype(jnp.bfloat16)
    right = (pmask * sig_b * lin_b).astype(jnp.bfloat16)
    blocks = 1
    left_four = left.reshape((blocks, hidden // blocks, row_count, crop_len))
    right_four = right.reshape((blocks, hidden // blocks, row_count, crop_len))
    left_ch, right_ch = (
        lax.all_to_all(left_four, "dap", split_axis=1, concat_axis=2, tiled=True),
        lax.all_to_all(right_four, "dap", split_axis=1, concat_axis=2, tiled=True),
    )
    tri_ch = triangle((left_ch, right_ch))
    tri_four = lax.all_to_all(tri_ch, "dap", split_axis=2, concat_axis=1, tiled=True)
    tri_rows = tri_four.reshape((hidden, row_count, crop_len))
    tri_f = tri_rows.astype(jnp.float32)
    tri_normed = norm_axis(tri_f, 0).astype(jnp.bfloat16)
    value = jnp.einsum("hrj,hc->rjc", tri_normed, w_out, preferred_element_type=jnp.float32)
    out_gate = jax.nn.sigmoid(
        jnp.einsum("rjc,cd->rjd", normed, w_gate, preferred_element_type=jnp.float32)
    )
    update = (out_gate * value).astype(jnp.bfloat16)
    cotan = d_out.astype(jnp.float32)
    d_value = (cotan * out_gate).astype(jnp.bfloat16)
    d_gate_pre = (cotan * value * out_gate * (1.0 - out_gate)).astype(jnp.bfloat16)
    grad_out = jnp.einsum("hrj,rjc->hc", tri_normed, d_value, preferred_element_type=jnp.float32)
    d_tn = jnp.einsum("rjc,hc->hrj", d_value, w_out, preferred_element_type=jnp.float32)
    d_tri = norm_back(d_tn, tri_f, 0).astype(jnp.bfloat16)
    d_tri_four = d_tri.reshape((blocks, hidden // blocks, row_count, crop_len))
    d_tri_ch = lax.all_to_all(d_tri_four, "dap", split_axis=1, concat_axis=2, tiled=True)
    d_left_ch = jnp.einsum(
        "qhkj,qhij->qhki", right_ch, d_tri_ch, preferred_element_type=jnp.float32
    ).astype(jnp.bfloat16)
    d_right_ch = jnp.einsum(
        "qhki,qhij->qhkj", left_ch, d_tri_ch, preferred_element_type=jnp.float32
    ).astype(jnp.bfloat16)
    d_left_four, d_right_four = (
        lax.all_to_all(d_left_ch, "dap", split_axis=2, concat_axis=1, tiled=True),
        lax.all_to_all(d_right_ch, "dap", split_axis=2, concat_axis=1, tiled=True),
    )
    d_left_f = d_left_four.reshape((hidden, row_count, crop_len)).astype(jnp.float32)
    d_right_f = d_right_four.reshape((hidden, row_count, crop_len)).astype(jnp.float32)
    pieces = [
        (d_left_f * pmask * sig_a).astype(jnp.bfloat16),
        (d_left_f * pmask * lin_a * sig_a * (1.0 - sig_a)).astype(jnp.bfloat16),
        (d_right_f * pmask * sig_b).astype(jnp.bfloat16),
        (d_right_f * pmask * lin_b * sig_b * (1.0 - sig_b)).astype(jnp.bfloat16),
    ]
    d_proj = jnp.concatenate(pieces, axis=0)
    grad_in = jnp.einsum("ric,hri->ch", normed, d_proj, preferred_element_type=jnp.float32)
    grad_gate = jnp.einsum("ric,rid->cd", normed, d_gate_pre, preferred_element_type=jnp.float32)
    d_normed = jnp.einsum("hri,ch->ric", d_proj, w_in, preferred_element_type=jnp.float32)
    d_normed = d_normed + jnp.einsum(
        "rid,cd->ric", d_gate_pre, w_gate, preferred_element_type=jnp.float32
    )
    d_pair = norm_back(d_normed, pair_f, -1).astype(jnp.bfloat16)
    total_in, total_gate, total_out = lax.psum((grad_in, grad_gate, grad_out), "dap")
    scale = jnp.float32(1.0 / crop_len)
    return (update, d_pair, total_in * scale, total_gate * scale, total_out * scale)


def solution(mesh):
    in_specs = (
        P(("groups", "dap"), None, None),
        P(("groups", "dap"), None, None),
        P("groups"),
        P(),
        P(),
        P(),
    )
    out_specs = (
        P(("groups", "dap"), None, None),
        P(("groups", "dap"), None, None),
        P("groups", None),
        P("groups", None),
        P("groups", None),
    )
    return jax.shard_map(shards, mesh=mesh, in_specs=in_specs, out_specs=out_specs, check_vma=False)
```

profile of v0, /device:TPU:0, one launch (start us, length us, event | category | flops | bytes accessed | tf_op | source)
XLA Modules:
  0.0 538.4 jit_solution(17067774272353493630)
XLA Ops:
  7.2 0.0 copy-start
  7.2 2.2 convert_reduce_fusion
  9.4 3.3 fusion.9
  12.7 4.3 add_divide_fusion
  16.9 4.3 add_divide_fusion.1
  21.3 1.9 fusion.50
  23.2 4.7 fusion.47
  27.9 0.1 dynamic_slice.3
  27.9 0.1 broadcast_multiply_fusion.3
  28.0 5.6 %fusion.37 = (bf16[1,128,20,320]{1,3,2,0:T(8,128)(2,1)}, bf16[1,128,20,320]{1,3,2,0:T(8,128)(2,1)}) fusion(f32[20,320,128]{2,1,0:T(8,128)} %fusion.47, f32[20,320,128]{2,1,0:T(8,128)} %add_divide_fusion, f32[20,320]{1,0:T(8,128)S(1)} %broadcast_multiply_fusion.3, f32[20,320,128]{2,1,0:T(8,128)S(1)} %fusion.50, f32[20,320,128]{2,1,0:T(8,128)} %add_divide_fusion.1), kind=kLoop, calls=%fused_computation.74 | loop fusion | flops 4915200 | bytes 16409600 | tf_op jit(solution)/shard_map/reshape | solution.py:52
  33.6 4.1 copy.42
  37.7 7.4 %all-to-all-start.1 = ((bf16[1,128,20,320]{3,2,0,1:T(8,128)(2,1)}), bf16[1,128,20,320]{3,2,0,1:T(8,128)(2,1)S(1)}, u32[]{:S(2)}, u32[]{:S(2)}) async-start(bf16[1,128,20,320]{3,2,0,1:T(8,128)(2,1)} %copy.42), calls=%async_computation.1 | async-start | bytes 4718592 | tf_op jit(solution)/shard_map/all_to_all | solution.py:55
  45.1 4.2 copy.39
  49.3 41.5 %all-to-all-done.1 = bf16[1,128,20,320]{3,2,0,1:T(8,128)(2,1)S(1)} async-done(((bf16[1,128,20,320]{3,2,0,1:T(8,128)(2,1)}), bf16[1,128,20,320]{3,2,0,1:T(8,128)(2,1)S(1)}, u32[]{:S(2)}, u32[]{:S(2)}) %all-to-all-start.1) | async-done | bytes 1638432 | tf_op jit(solution)/shard_map/all_to_all | solution.py:55
  90.8 12.3 %all-to-all-start = ((bf16[1,128,20,320]{3,2,0,1:T(8,128)(2,1)}), bf16[1,128,20,320]{3,2,0,1:T(8,128)(2,1)}, u32[]{:S(2)}, u32[]{:S(2)}) async-start(bf16[1,128,20,320]{3,2,0,1:T(8,128)(2,1)} %copy.39), calls=%async_computation | async-start | bytes 4718592 | tf_op jit(solution)/shard_map/all_to_all | solution.py:54
  103.1 0.3 copy.85
  103.4 0.2 copy.44
  103.7 45.2 %all-to-all-done = bf16[1,128,20,320]{3,2,0,1:T(8,128)(2,1)} async-done(((bf16[1,128,20,320]{3,2,0,1:T(8,128)(2,1)}), bf16[1,128,20,320]{3,2,0,1:T(8,128)(2,1)}, u32[]{:S(2)}, u32[]{:S(2)}) %all-to-all-start) | async-done | bytes 1638432 | tf_op jit(solution)/shard_map/all_to_all | solution.py:54
  148.8 2.0 copy.86
  150.8 0.2 copy.41
  151.1 1.6 convert_bitcast_fusion.5
  152.7 1.2 copy.47
  153.8 57.1 %all_to_all.72 = bf16[1,8,320,320]{3,1,0,2:T(8,128)(2,1)S(1)} all-to-all(bf16[1,8,320,320]{3,1,0,2:T(8,128)(2,1)S(1)} %copy.47), channel_id=1, replica_groups=mesh['groups'=2,'dap'=16] {'dap'}, dimensions={2} | all-to-all | bytes 3276800 | tf_op jit(solution)/shard_map/all_to_all | solution.py:58
  210.9 0.4 fusion.29
  211.3 2.3 copy_bitcast_fusion.2
  213.6 0.6 multiply_reduce_fusion
  214.2 3.6 copy.50
  217.9 3.9 fusion.41
  221.8 4.3 fusion.13
  226.0 5.0 bitcast_reduce_fusion
  231.1 5.9 %fusion.38 = bf16[1,128,20,320]{1,3,2,0:T(8,128)(2,1)} fusion(f32[128,20,320]{0,2,1:T(8,128)S(1)} %copy.50, f32[20,320,128]{2,1,0:T(8,128)S(1)} %get-tuple-element.23, f32[20,320]{1,0:T(8,128)S(1)} %get-tuple-element.25, f32[20,320]{1,0:T(8,128)S(1)} %get-tuple-element.26, f32[20,320]{1,0:T(8,128)S(1)} %add_rsqrt_fusion, ...), kind=kLoop, calls=%fused_computation.75 | loop fusion | flops 5734400 | bytes 8294400 | tf_op jit(solution)/shard_map/reshape | solution.py:73
  236.9 4.1 copy.51
  241.0 58.5 %all_to_all.73 = bf16[1,128,20,320]{3,2,0,1:T(8,128)(2,1)S(1)} all-to-all(bf16[1,128,20,320]{3,2,0,1:T(8,128)(2,1)} %copy.51), channel_id=1, replica_groups=mesh['groups'=2,'dap'=16] {'dap'}, dimensions={1} | all-to-all | bytes 3276800 | tf_op jit(solution)/shard_map/all_to_all | solution.py:74
  299.6 0.3 copy.84
  299.9 0.2 copy.53
  300.1 1.1 copy-done.10
  301.2 1.5 convert_bitcast_fusion.3
  302.7 2.5 copy.62
  305.1 4.4 all-to-all-start.5
  309.6 3.6 convert_bitcast_fusion.4
  313.2 2.5 copy.56
  315.6 32.8 %all-to-all-done.5 = bf16[1,8,320,320]{3,1,0,2:T(8,128)(2,1)} async-done(((bf16[1,8,320,320]{3,1,0,2:T(8,128)(2,1)}), bf16[1,8,320,320]{3,1,0,2:T(8,128)(2,1)}, u32[]{:S(2)}, u32[]{:S(2)}) %all-to-all-start.5) | async-done | bytes 1638432 | tf_op jit(solution)/shard_map/all_to_all | solution.py:83
  348.4 10.7 %all-to-all-start.4 = ((bf16[1,8,320,320]{3,1,0,2:T(8,128)(2,1)}), bf16[1,8,320,320]{3,1,0,2:T(8,128)(2,1)}, u32[]{:S(2)}, u32[]{:S(2)}) async-start(bf16[1,8,320,320]{3,1,0,2:T(8,128)(2,1)} %copy.56), calls=%async_computation.4 | async-start | bytes 3932160 | tf_op jit(solution)/shard_map/all_to_all | solution.py:82
  359.1 0.3 all-reduce.3.cloned.1.call-start
  359.4 4.9 convolution_bitcast_fusion.2
  364.3 4.7 convolution_bitcast_fusion.1
  369.1 3.8 copy_bitcast_fusion
  372.9 5.2 copy.65
  378.1 19.9 %all-to-all-done.4 = bf16[1,8,320,320]{3,1,0,2:T(8,128)(2,1)} async-done(((bf16[1,8,320,320]{3,1,0,2:T(8,128)(2,1)}), bf16[1,8,320,320]{3,1,0,2:T(8,128)(2,1)}, u32[]{:S(2)}, u32[]{:S(2)}) %all-to-all-start.4) | async-done | bytes 1638432 | tf_op jit(solution)/shard_map/all_to_all | solution.py:82
  398.0 3.8 copy_bitcast_fusion.1
  401.8 5.3 copy.59
  407.1 8.1 %fusion.27 = (bf16[128,20,320]{0,2,1:T(8,128)(2,1)S(1)}, bf16[128,20,320]{0,2,1:T(8,128)(2,1)S(1)}, bf16[128,20,320]{0,2,1:T(8,128)(2,1)S(1)}, bf16[128,20,320]{0,2,1:T(8,128)(2,1)S(1)}) fusion(f32[20,320,128]{2,1,0:T(8,128)} %add_divide_fusion.1, f32[128,20,320]{0,2,1:T(8,128)} %copy.59, f32[20,320]{1,0:T(8,128)S(1)} %broadcast_multiply_fusion.3, ...), kind=kLoop, calls=%fused_computation.52 | loop fusion | flops 13107200 | bytes 26240000 | tf_op jit(solution)/shard_map/convert_element_type | solution.py:88
  415.2 1.2 copy-done.13
  416.4 0.5 copy-done.14
  416.9 0.5 copy-done.15
  417.4 3.4 convolution_bitcast_fusion
  420.8 3.9 fusion.39
  424.7 5.1 fusion.70
  429.8 0.0 all-reduce.3.cloned.1.call-update
  429.8 8.6 %fusion.8 = bf16[20,320,128]{2,1,0:T(8,128)(2,1)} fusion(bf16[20,320,128]{2,1,0:T(8,128)(2,1)S(1)} %copy-done.3, f32[20,320,128]{2,1,0:T(8,128)} %get-tuple-element.24, f32[20,320]{1,0:T(8,128)S(1)} %broadcast_multiply_fusion.4, f32[20,320]{1,0:T(8,128)S(1)} %broadcast_multiply_fusion.5, f32[20,320]{1,0:T(8,128)S(1)} %add_rsqrt_fusion.1, ...), kind=kLoop, calls=%fused_computation.20 | loop fusion | flops 6553600 | bytes 6656000 | tf_op jit(solution)/shard_map/convert_element_type | solution.py:100
  438.4 88.5 %all-reduce.3.cloned.1.call-done = (f32[128,512]{1,0:T(8,128)}, f32[128,128]{1,0:T(8,128)}, f32[128,128]{1,0:T(8,128)}) async-done(((f32[128,512]{1,0:T(8,128)}, f32[128,128]{1,0:T(8,128)}, f32[128,128]{1,0:T(8,128)}), (f32[128,512]{1,0:T(8,128)}, f32[128,128]{1,0:T(8,128)}, f32[128,128]{1,0:T(8,128)})) %all-reduce.3.cloned.1.call-update) | async-done | bytes 393232 | tf_op jit(solution)/shard_map/psum | solution.py:101
  526.9 1.7 broadcast_multiply_fusion
  528.6 1.5 broadcast_multiply_fusion.1
  530.1 1.5 broadcast_multiply_fusion.2
  (43 shorter events, 0.1 us)
Async XLA Ops:
  7.2 214.6 %copy-start = (bf16[128,128]{1,0:T(8,128)(2,1)S(1)}, bf16[128,128]{1,0:T(8,128)(2,1)}, u32[]{:S(2)}) copy-start(bf16[128,128]{1,0:T(8,128)(2,1)} %param.10) | copy-start | bytes 98308
  7.2 5.5 %copy-start.1 = (bf16[20,320,128]{2,1,0:T(8,128)(2,1)S(1)}, bf16[20,320,128]{2,1,0:T(8,128)(2,1)}, u32[]{:S(2)}) copy-start(bf16[20,320,128]{2,1,0:T(8,128)(2,1)} %param.6) | copy-start | bytes 4915204
  7.2 5.5 %copy-start.17 = (bf16[128,512]{1,0:T(8,128)(2,1)S(1)}, bf16[128,512]{1,0:T(8,128)(2,1)}, u32[]{:S(2)}) copy-start(bf16[128,512]{1,0:T(8,128)(2,1)} %param.9) | copy-start | bytes 393220
  23.1 10.5 %copy-start.4 = (f32[20,320,128]{2,1,0:T(8,128)}, f32[20,320,128]{2,1,0:T(8,128)S(1)}, u32[]{:S(2)}) copy-start(f32[20,320,128]{2,1,0:T(8,128)S(1)} %fusion.50) | copy-start | bytes 9830404
  23.1 4.7 copy-start.19
  37.7 53.1 %all-to-all-start.1 = ((bf16[1,128,20,320]{3,2,0,1:T(8,128)(2,1)}), bf16[1,128,20,320]{3,2,0,1:T(8,128)(2,1)S(1)}, u32[]{:S(2)}, u32[]{:S(2)}) async-start(bf16[1,128,20,320]{3,2,0,1:T(8,128)(2,1)} %copy.42), calls=%async_computation.1 | async-start | bytes 4718592 | tf_op jit(solution)/shard_map/all_to_all | solution.py:55
  90.8 58.1 %all-to-all-start = ((bf16[1,128,20,320]{3,2,0,1:T(8,128)(2,1)}), bf16[1,128,20,320]{3,2,0,1:T(8,128)(2,1)}, u32[]{:S(2)}, u32[]{:S(2)}) async-start(bf16[1,128,20,320]{3,2,0,1:T(8,128)(2,1)} %copy.39), calls=%async_computation | async-start | bytes 4718592 | tf_op jit(solution)/shard_map/all_to_all | solution.py:54
  103.6 47.4 %copy-start.8 = (bf16[1,8,16,20,320]{4,1,3,2,0:T(8,128)(2,1)}, bf16[1,8,16,20,320]{4,1,3,2,0:T(8,128)(2,1)S(1)}, u32[]{:S(2)}) copy-start(bf16[1,8,16,20,320]{4,1,3,2,0:T(8,128)(2,1)S(1)} %copy.44) | copy-start | bytes 4915204
  151.0 2.8 copy-start.9
  214.2 3.6 copy-start.16
  217.8 3.9 copy-start.2
  217.9 3.9 copy-start.7
  226.0 5.0 copy-start.5
  299.6 1.6 copy-start.10
  300.1 2.6 copy-start.11
  305.1 43.2 %all-to-all-start.5 = ((bf16[1,8,320,320]{3,1,0,2:T(8,128)(2,1)}), bf16[1,8,320,320]{3,1,0,2:T(8,128)(2,1)}, u32[]{:S(2)}, u32[]{:S(2)}) async-start(bf16[1,8,320,320]{3,1,0,2:T(8,128)(2,1)} %copy.62), calls=%async_computation.5 | async-start | bytes 3932160 | tf_op jit(solution)/shard_map/all_to_all | solution.py:83
  348.4 49.6 %all-to-all-start.4 = ((bf16[1,8,320,320]{3,1,0,2:T(8,128)(2,1)}), bf16[1,8,320,320]{3,1,0,2:T(8,128)(2,1)}, u32[]{:S(2)}, u32[]{:S(2)}) async-start(bf16[1,8,320,320]{3,1,0,2:T(8,128)(2,1)} %copy.56), calls=%async_computation.4 | async-start | bytes 3932160 | tf_op jit(solution)/shard_map/all_to_all | solution.py:82
  359.1 167.8 %all-reduce.3.cloned.1.call-start = ((), (), s32[]{:S(2)}) async-start(), calls=%async_computation.6 | async-start | bytes 786432 | tf_op jit(solution)/shard_map/psum | solution.py:101
  359.4 5.0 copy-start.6
  407.1 10.3 %copy-start.3 = (bf16[20,320,128]{2,1,0:T(8,128)(2,1)S(1)}, bf16[20,320,128]{2,1,0:T(8,128)(2,1)}, u32[]{:S(2)}) copy-start(bf16[20,320,128]{2,1,0:T(8,128)(2,1)} %param.6) | copy-start | bytes 4915204
  415.2 1.2 copy-start.13
  415.2 1.7 copy-start.14
  415.2 2.2 copy-start.15
  417.4 3.4 copy-start.18
  420.8 3.9 copy-start.12
Sparse Core Ops, SparseCore 0:
  429.9 96.9 all-reduce.2
where the time goes:
time: 540 us; the launch traced here: 538 us
  waiting for transfers between devices  228 us (42%)
  blocking collectives  116 us (21%)
  matrix products  57 us (11%)
  other arithmetic  49.2 us (9%)
  local copies, waits for them, and re-layouts  39.2 us (7%)
  starting transfers between devices  35.1 us (6%)
  between operations  14.4 us (3%)
    psum x1, waiting for transfers between devices, shards(): lax.psum((grad_in, grad_gate, grad_out), 'dap')  88.5 us
    all_to_all x1, blocking collectives, shards(): lax.all_to_all(d_tri_four, 'dap', split_axis=1, concat_axis=2, tiled=True)  58.5 us
    all_to_all x1, blocking collectives, shards(): lax.all_to_all(tri_ch, 'dap', split_axis=2, concat_axis=1, tiled=True)  57.1 us
    all_to_all x1, waiting for transfers between devices, shards(): lax.all_to_all(left_four, 'dap', split_axis=1, concat_axis=2, tiled=True)  45.2 us
    all_to_all x1, waiting for transfers between devices, shards(): lax.all_to_all(right_four, 'dap', split_axis=1, concat_axis=2, tiled=True)  41.5 us
    all_to_all x1, waiting for transfers between devices, shards(): lax.all_to_all(d_right_ch, 'dap', split_axis=2, concat_axis=1, tiled=True)  32.8 us
    all_to_all x1, waiting for transfers between devices, shards(): lax.all_to_all(d_left_ch, 'dap', split_axis=2, concat_axis=1, tiled=True)  19.9 us
    dot_general x4, matrix products, project(): jnp.einsum('ric,ch->hri', normed, weight, preferred_element_type=jnp.floa...  15.2 us
  transfers between devices with their start and end apart: 5, of which 5 were waited for; matrix products, arithmetic and copies ran while one was open for 7% of the time, Pallas kernels for 0%

commit v1 on v0

v1 whole, which is shorter than its diff:
```python
import functools
import math

import jax
import jax.numpy as jnp
from jax import lax
from jax.experimental import pallas as pl
from jax.experimental.pallas import tpu as pltpu
from jax.sharding import PartitionSpec as P

F32 = jnp.float32
BF16 = jnp.bfloat16
EPS = 1e-05
AXIS = "dap"


def greet(n):
    me = lax.axis_index(AXIS)
    barrier = pltpu.get_barrier_semaphore()

    def one(step, carry):
        peer = lax.rem(me + step, n)
        pl.semaphore_signal(barrier, inc=1, device_id={AXIS: peer}, device_id_type=pl.DeviceIdType.MESH)
        return carry

    lax.fori_loop(1, n, one, 0)
    pl.semaphore_wait(barrier, n - 1)


def push(src, dst, send_sem, recv_sem, peer):
    return pltpu.make_async_remote_copy(
        src_ref=src,
        dst_ref=dst,
        send_sem=send_sem,
        recv_sem=recv_sem,
        device_id={AXIS: peer},
        device_id_type=pl.DeviceIdType.MESH,
    )


def push_chunk(n, c, src, dst, send_sem, recv_sem):
    me = lax.axis_index(AXIS)

    def one(step, carry):
        peer = lax.rem(me + step, n)
        push(src.at[peer, c], dst.at[me, c], send_sem.at[c, peer], recv_sem.at[c, me], peer).start()
        return carry

    lax.fori_loop(1, n, one, 0)


def await_recv(n, c, src, dst, send_sem, recv_sem):
    me = lax.axis_index(AXIS)

    def one(step, carry):
        peer = lax.rem(me + n - step, n)
        push(src.at[peer, c], dst.at[peer, c], send_sem.at[c, peer], recv_sem.at[c, peer], peer).wait_recv()
        return carry

    lax.fori_loop(1, n, one, 0)


def await_send(n, c, src, dst, send_sem, recv_sem):
    me = lax.axis_index(AXIS)

    def one(step, carry):
        peer = lax.rem(me + step, n)
        push(src.at[peer, c], dst.at[me, c], send_sem.at[c, peer], recv_sem.at[c, me], peer).wait_send()
        return carry

    lax.fori_loop(1, n, one, 0)


def dot(a, b, da, db):
    return lax.dot_general(a, b, (((da,), (db,)), ((), ())), preferred_element_type=F32)


def loop(count, body):
    def step(c, carry):
        body(c)
        return carry

    lax.fori_loop(0, count, step, 0)


def first_kernel(n, chunks, group, pair_ref, mask_ref, w_ref, normed_ref, out_ref, send, send_sem, recv_sem, own_sem):
    me = lax.axis_index(AXIS)
    greet(n)
    half = w_ref.shape[0] // 2
    rows = half // n
    width = pair_ref.shape[1]

    def body(c):
        for j in range(group):
            q = c * group + j
            x = pair_ref[q].astype(F32)
            center = x - jnp.mean(x, axis=-1, keepdims=True)
            inverse = lax.rsqrt(jnp.mean(center * center, axis=-1, keepdims=True) + EPS)
            normed = (center * inverse).astype(BF16)
            normed_ref[q] = normed
            lin = dot(w_ref[0:half, :], normed, 1, 1)
            gate = dot(w_ref[half:, :], normed, 1, 1)
            gated = (mask_ref[q] * jax.nn.sigmoid(gate) * lin).reshape((n, rows, width))
            send[:, c, j * rows : (j + 1) * rows, :] = gated.astype(BF16)
        push_chunk(n, c, send, out_ref, send_sem, recv_sem)

    loop(chunks, body)
    own = pltpu.make_async_copy(send.at[me], out_ref.at[me], own_sem)
    own.start()
    loop(chunks, lambda c: await_send(n, c, send, out_ref, send_sem, recv_sem))
    loop(chunks, lambda c: await_recv(n, c, send, out_ref, send_sem, recv_sem))
    own.wait()


def middle_kernel(
    n, chunks, group,
    tri_ref, normed_ref, cotan_ref, w_gate_ref, w_out_ref,
    update_ref, dgp_ref, grad_ref, out_ref,
    recv, send, in_send_sem, in_recv_sem, send_sem, recv_sem, own_sem,
):
    me = lax.axis_index(AXIS)
    greet(n)
    loop(chunks, lambda c: push_chunk(n, c, tri_ref, recv, in_send_sem, in_recv_sem))
    own_in = pltpu.make_async_copy(tri_ref.at[me], recv.at[me], own_sem.at[0])
    own_in.start()
    hidden = w_out_ref.shape[0]
    rows = hidden // n
    width = normed_ref.shape[1]
    grad_ref[...] = jnp.zeros_like(grad_ref)
    own_in.wait()

    def body(c):
        await_recv(n, c, tri_ref, recv, in_send_sem, in_recv_sem)
        block = recv[:, c].astype(F32)
        parts = []
        for j in range(group):
            q = c * group + j
            tri = block[:, j * rows : (j + 1) * rows, :].reshape((hidden, width))
            center = tri - jnp.mean(tri, axis=0, keepdims=True)
            inverse = lax.rsqrt(jnp.mean(center * center, axis=0, keepdims=True) + EPS)
            hat = center * inverse
            tri_normed = hat.astype(BF16)
            value = dot(tri_normed, w_out_ref[...], 0, 0)
            normed = normed_ref[q]
            out_gate = jax.nn.sigmoid(dot(normed, w_gate_ref[...], 1, 0))
            cotan = cotan_ref[q].astype(F32)
            update_ref[q] = (out_gate * value).astype(BF16)
            d_value = (cotan * out_gate).astype(BF16)
            dgp = (cotan * value * out_gate * (1.0 - out_gate)).astype(BF16)
            dgp_ref[q] = dgp
            grad_ref[0:hidden, :] += dot(tri_normed, d_value, 1, 0)
            grad_ref[hidden:, :] += dot(normed, dgp, 0, 0)
            d_tn = dot(w_out_ref[...], d_value, 1, 1)
            shifted = d_tn - jnp.mean(d_tn, axis=0, keepdims=True)
            d_tri = inverse * (shifted - hat * jnp.mean(d_tn * hat, axis=0, keepdims=True))
            parts.append(d_tri.reshape((n, rows, width)))
        send[:, c] = jnp.concatenate(parts, axis=1).astype(BF16)
        push_chunk(n, c, send, out_ref, send_sem, recv_sem)

    loop(chunks, body)
    own = pltpu.make_async_copy(send.at[me], out_ref.at[me], own_sem.at[1])
    own.start()
    loop(chunks, lambda c: await_send(n, c, tri_ref, recv, in_send_sem, in_recv_sem))
    loop(chunks, lambda c: await_send(n, c, send, out_ref, send_sem, recv_sem))
    loop(chunks, lambda c: await_recv(n, c, send, out_ref, send_sem, recv_sem))
    own.wait()


def last_kernel(
    n, chunks, group, scale,
    dlr_ref, pair_ref, normed_ref, dgp_ref, mask_ref, w_t_ref, w_ref, w_gate_ref, grad_ref,
    d_pair_ref, total_ref,
    recv, grads, slices, in_send_sem, in_recv_sem, rs_send, rs_recv, ag_send, ag_recv, own_sem,
):
    me = lax.axis_index(AXIS)
    greet(n)
    loop(chunks, lambda c: push_chunk(n, c, dlr_ref, recv, in_send_sem, in_recv_sem))
    own_in = pltpu.make_async_copy(dlr_ref.at[me], recv.at[me], own_sem)
    own_in.start()
    full = w_t_ref.shape[0]
    half = full // 2
    rows = half // n
    width = pair_ref.shape[1]
    part = slices.shape[1]
    channels = w_ref.shape[0]
    own_in.wait()

    def body(c):
        await_recv(n, c, dlr_ref, recv, in_send_sem, in_recv_sem)
        block = recv[:, c].astype(F32)
        for j in range(group):
            q = c * group + j
            cotan = block[:, j * rows : (j + 1) * rows, :].reshape((half, width)) * mask_ref[q]
            normed = normed_ref[q]
            lin = dot(w_t_ref[0:half, :], normed, 1, 1)
            sig = jax.nn.sigmoid(dot(w_t_ref[half:, :], normed, 1, 1))
            d_lin = cotan * sig
            d_gate = (d_lin * lin * (1.0 - sig)).astype(BF16)
            d_lin = d_lin.astype(BF16)
            grads[0:half, :] += dot(d_lin, normed, 1, 0)
            grads[half:full, :] += dot(d_gate, normed, 1, 0)
            d_normed = dot(w_ref[:, 0:half], d_lin, 1, 0) + dot(w_ref[:, half:], d_gate, 1, 0)
            d_normed = d_normed.T + dot(dgp_ref[q], w_gate_ref[...], 1, 1)
            x = pair_ref[q].astype(F32)
            center = x - jnp.mean(x, axis=-1, keepdims=True)
            inverse = lax.rsqrt(jnp.mean(center * center, axis=-1, keepdims=True) + EPS)
            hat = center * inverse
            shifted = d_normed - jnp.mean(d_normed, axis=-1, keepdims=True)
            d_pair = inverse * (shifted - hat * jnp.mean(d_normed * hat, axis=-1, keepdims=True))
            d_pair_ref[q] = d_pair.astype(BF16)

    grads[0:full, :] = jnp.zeros((full, channels), F32)
    grads[full:, :] = grad_ref[...]
    loop(chunks, body)

    def own_rows(d):
        return grads.at[pl.ds(pl.multiple_of(d * part, 8), part), :]

    def scatter(step, carry):
        peer = lax.rem(me + step, n)
        push(own_rows(peer), slices.at[me], rs_send.at[peer], rs_recv.at[me], peer).start()
        return carry

    lax.fori_loop(1, n, scatter, 0)
    slices[me] = grads[pl.ds(pl.multiple_of(me * part, 8), part), :]

    def scattered(step, carry):
        peer = lax.rem(me + n - step, n)
        push(own_rows(peer), slices.at[peer], rs_send.at[peer], rs_recv.at[peer], peer).wait_recv()
        return carry

    lax.fori_loop(1, n, scattered, 0)
    total = slices[0]
    for d in range(1, n):
        total = total + slices[d]
    total_ref[me] = total * scale

    def gather(step, carry):
        peer = lax.rem(me + step, n)
        push(total_ref.at[me], total_ref.at[me], ag_send.at[peer], ag_recv.at[me], peer).start()
        return carry

    lax.fori_loop(1, n, gather, 0)

    def gathered(step, carry):
        peer = lax.rem(me + n - step, n)
        push(total_ref.at[me], total_ref.at[peer], ag_send.at[peer], ag_recv.at[peer], peer).wait_recv()
        return carry

    lax.fori_loop(1, n, gathered, 0)

    def sent(step, carry):
        peer = lax.rem(me + step, n)
        push(own_rows(peer), slices.at[me], rs_send.at[peer], rs_recv.at[me], peer).wait_send()
        push(total_ref.at[me], total_ref.at[me], ag_send.at[peer], ag_recv.at[me], peer).wait_send()
        return carry

    lax.fori_loop(1, n, sent, 0)
    loop(chunks, lambda c: await_send(n, c, dlr_ref, recv, in_send_sem, in_recv_sem))


VMEM = pl.BlockSpec(memory_space=pltpu.VMEM)
ANY = pl.BlockSpec(memory_space=pl.ANY)
DMA = pltpu.SemaphoreType.DMA


def params(which):
    return pltpu.CompilerParams(collective_id=which, has_side_effects=True, vmem_limit_bytes=50 * 1024 * 1024)


def shards(n, pair, d_out, residue_mask, w_in, w_gate, w_out):
    row_count, crop, channels = pair.shape
    hidden = w_out.shape[0]
    hd = hidden // n
    fold = 128 // math.gcd(128, crop)
    width = fold * crop
    steps = row_count // fold
    me = lax.axis_index(AXIS)
    mask_all = residue_mask.astype(F32)
    mask_rows = lax.dynamic_slice_in_dim(mask_all, me * row_count, row_count, 0)
    pmask = (mask_rows[:, None] * mask_all[None, :]).reshape((steps, 1, width))
    w_perm = w_in.reshape((channels, 2, 2, n, hd)).transpose((0, 2, 3, 1, 4)).reshape((channels, 4 * hidden))
    w_perm_t = w_perm.T
    pair_q = pair.reshape((steps, width, channels))
    cotan_q = d_out.reshape((steps, width, channels))

    group = 32 // (2 * hd)
    chunks = steps // group
    lr_shape = (n, chunks, group * 2 * hd, width)
    normed, lr = pl.pallas_call(
        functools.partial(first_kernel, n, chunks, group),
        name="project_and_send",
        out_shape=(
            jax.ShapeDtypeStruct((steps, width, channels), BF16),
            jax.ShapeDtypeStruct(lr_shape, BF16),
        ),
        in_specs=[VMEM] * 3,
        out_specs=(VMEM, ANY),
        scratch_shapes=[pltpu.VMEM(lr_shape, BF16), DMA((chunks, n)), DMA((chunks, n)), DMA],
        compiler_params=params(0),
    )(pair_q, pmask, w_perm_t)

    lr = lr.reshape((n, steps, 2, hd, fold, crop)).transpose((2, 3, 0, 1, 4, 5)).reshape((2, hd, n * row_count, crop))
    left, right = lr[0], lr[1]
    tri = jnp.einsum("hki,hkj->hij", left, right, preferred_element_type=F32).astype(BF16)
    group3 = 16 // hd
    chunks3 = steps // group3
    tri_shape = (n, chunks3, group3 * hd, width)
    tri = tri.reshape((hd, n, steps, fold, crop)).transpose((1, 2, 0, 3, 4)).reshape(tri_shape)

    update, dgp, grads, d_tri = pl.pallas_call(
        functools.partial(middle_kernel, n, chunks3, group3),
        name="gate_and_back",
        out_shape=(
            jax.ShapeDtypeStruct((steps, width, channels), BF16),
            jax.ShapeDtypeStruct((steps, width, channels), BF16),
            jax.ShapeDtypeStruct((hidden + channels, channels), F32),
            jax.ShapeDtypeStruct(tri_shape, BF16),
        ),
        in_specs=[ANY] + [VMEM] * 4,
        out_specs=(VMEM, VMEM, VMEM, ANY),
        scratch_shapes=[
            pltpu.VMEM(tri_shape, BF16),
            pltpu.VMEM(tri_shape, BF16),
            DMA((chunks3, n)),
            DMA((chunks3, n)),
            DMA((chunks3, n)),
            DMA((chunks3, n)),
            DMA((2,)),
        ],
        compiler_params=params(1),
    )(tri, normed, cotan_q, w_gate, w_out)

    d_tri = d_tri.reshape((n, steps, hd, fold, crop)).transpose((2, 0, 1, 3, 4)).reshape((hd, n * row_count, crop))
    d_left = jnp.einsum("hkj,hij->hki", right, d_tri, preferred_element_type=F32).astype(BF16)
    d_right = jnp.einsum("hki,hij->hkj", left, d_tri, preferred_element_type=F32).astype(BF16)
    dlr = jnp.stack([d_left, d_right]).reshape((2, hd, n, steps, fold, crop))
    dlr = dlr.transpose((2, 3, 0, 1, 4, 5)).reshape(lr_shape)

    grad_rows = 4 * hidden + hidden + channels
    part = grad_rows // n
    d_pair, total = pl.pallas_call(
        functools.partial(last_kernel, n, chunks, group, 1.0 / crop),
        name="pair_gradient",
        out_shape=(
            jax.ShapeDtypeStruct((steps, width, channels), BF16),
            jax.ShapeDtypeStruct((n, part, channels), F32),
        ),
        in_specs=[ANY] + [VMEM] * 8,
        out_specs=(VMEM, VMEM),
        scratch_shapes=[
            pltpu.VMEM(lr_shape, BF16),
            pltpu.VMEM((grad_rows, channels), F32),
            pltpu.VMEM((n, part, channels), F32),
            DMA((chunks, n)),
            DMA((chunks, n)),
            DMA((n,)),
            DMA((n,)),
            DMA((n,)),
            DMA((n,)),
            DMA,
        ],
        compiler_params=params(2),
    )(dlr, pair_q, normed, dgp, pmask, w_perm_t, w_perm, w_gate, grads)

    total = total.reshape((grad_rows, channels))
    total_in = total[: 4 * hidden].reshape((2, n, 2, hd, channels)).transpose((4, 2, 0, 1, 3))
    total_in = total_in.reshape((channels, 4 * hidden))
    return (
        update.reshape(pair.shape),
        d_pair.reshape(pair.shape),
        total_in,
        total[5 * hidden :],
        total[4 * hidden : 5 * hidden],
    )


def solution(mesh):
    in_specs = (
        P(("groups", "dap"), None, None),
        P(("groups", "dap"), None, None),
        P("groups"),
        P(),
        P(),
        P(),
    )
    out_specs = (
        P(("groups", "dap"), None, None),
        P(("groups", "dap"), None, None),
        P("groups", None),
        P("groups", None),
        P("groups", None),
    )
    body = functools.partial(shards, mesh.shape[AXIS])
    return jax.shard_map(body, mesh=mesh, in_specs=in_specs, out_specs=out_specs, check_vma=False)
```

time: 540 us -> 358 us (0.66)
  Pallas kernels: 0 us -> 256 us
  waiting for transfers between devices: 228 us -> 0 us
  blocking collectives: 116 us -> 0 us
  matrix products: 57 us -> 12.4 us
  other arithmetic: 49.2 us -> 8.91 us
  local copies, waits for them, and re-layouts: 39.2 us -> 75.8 us
  starting transfers between devices: 35.1 us -> 0 us
  between operations: 14.4 us -> 0.82 us
    pallas_call x0 -> x3, Pallas kernels: none -> 256 us  [the longest x1 98.8 us: shards(): pl.pallas_call(functools.partial(last_kernel, n, chunks, group, 1.0 / cro...]
    all_to_all x4 -> x0, waiting for transfers between devices: 139 us -> none  [the longest x1 45.2 us: shards(): lax.all_to_all(left_four, 'dap', split_axis=1, concat_axis=2, tiled=True)]
    all_to_all x2 -> x0, blocking collectives: 116 us -> none  [the longest x1 58.5 us: shards(): lax.all_to_all(d_tri_four, 'dap', split_axis=1, concat_axis=2, tiled=True)]
    psum x1 -> x0, waiting for transfers between devices: 88.5 us -> none  [shards(): lax.psum((grad_in, grad_gate, grad_out), 'dap')]
    dot_general x15 -> x3, matrix products: 57 us -> 12.4 us  [the longest x1 4.79 us: shards(): jnp.einsum('hkj,hij->hki', right, d_tri, preferred_element_type=F32)]
    all_to_all x4 -> x0, starting transfers between devices: 34.8 us -> none  [the longest x1 12.3 us: shards(): lax.all_to_all(left_four, 'dap', split_axis=1, concat_axis=2, tiled=True)]
    reshape x3 -> x9, local copies, waits for them, and re-layouts: 12.4 us -> 43.3 us  [the longest x2 12 us: shards(): lr.reshape((n, steps, 2, hd, fold, crop)).transpose((2, 3, 0, 1, 4, 5))]
    convert_element_type x6 -> x1, other arithmetic: 26.6 us -> 0.68 us  [shards(): mask_all = residue_mask.astype(F32)]
  transfers between devices with their start and end apart: 5 -> 0, of which waited for: 5 -> 0; matrix products, arithmetic and copies ran while one was open for 7% -> 0% of each run, Pallas kernels for 0% -> 0%
where the time goes in v1:
time: 358 us; the launch traced here: 354 us
  Pallas kernels  256 us (72%)
  local copies, waits for them, and re-layouts  75.8 us (21%)
  matrix products  12.4 us (3%)
  other arithmetic  8.91 us (2%)
    pallas_call x1, Pallas kernels, shards(): pl.pallas_call(functools.partial(last_kernel, n, chunks, group, 1.0 / cro...  98.8 us
    pallas_call x1, Pallas kernels, shards(): pl.pallas_call(functools.partial(middle_kernel, n, chunks3, group3), name...  83 us
    pallas_call x1, Pallas kernels, shards(): pl.pallas_call(functools.partial(first_kernel, n, chunks, group), name='p...  74.3 us
    unnamed x36, local copies, waits for them, and re-layouts  15.1 us
    reshape x2, local copies, waits for them, and re-layouts, shards(): lr.reshape((n, steps, 2, hd, fold, crop)).transpose((2, 3, 0, 1, 4, 5))  12 us
    reshape x3, local copies, waits for them, and re-layouts, shards(): tri.reshape((hd, n, steps, fold, crop)).transpose((1, 2, 0, 3, 4))  11.8 us
    reshape x2, local copies, waits for them, and re-layouts, shards(): d_tri.reshape((n, steps, hd, fold, crop)).transpose((2, 0, 1, 3, 4))  10.5 us
    another operation x2, local copies, waits for them, and re-layouts, shards(): dlr = jnp.stack([d_left, d_right]).reshape((2, hd, n, steps, fold, crop))  10.1 us

profile of v1, /device:TPU:0, one launch (start us, length us, event | category | flops | bytes accessed | tf_op | source)
XLA Modules:
  0.0 354.1 jit_solution(952987485595450393)
XLA Ops:
  0.6 0.7 convert_element_type.12
  1.3 0.1 dynamic_slice.3
  1.4 0.1 mul.32
  1.5 0.1 mul.33
  1.6 0.1 mul.34
  1.7 0.1 mul.36
  1.8 0.0 copy-start.7
  1.8 1.0 copy.34
  2.9 0.0 copy-start
  2.9 1.4 copy-done
  4.3 74.3 %project_and_send.1 = (bf16[10,640,128]{2,1,0:T(8,128)(2,1)S(1)}, bf16[16,5,32,640]{3,2,1,0:T(8,128)(2,1)}) custom-call(bf16[10,640,128]{2,1,0:T(8,128)(2,1)S(1)} %bitcast.32, f32[10,1,640]{2,1,0:T(1,128)S(1)} %broadcast_multiply_fusion.mask_ref, bf16[512,128]{1,0:T(8,128)(2,1)S(1)} %bitcast.34), custom_call_target="tpu_custom_call" | custom-call | tf_op jit(solution)/shard_map/project_and_send/pallas_call | solution.py:290
  78.6 0.0 copy-start.2
  78.7 1.2 copy-done.2
  79.8 9.2 %reshape.110 = bf16[16,10,2,8,2,320]{5,4,3,2,1,0:T(2,128)(2,1)} reshape(bf16[16,5,32,640]{3,2,1,0:T(8,128)(2,1)} %get-tuple-element.13) | data formatting | bytes 6553600 | tf_op jit(solution)/shard_map/reshape | solution.py:303
  89.0 0.0 copy-done.7
  89.0 2.8 copy.60
  91.8 0.4 fusion.4
  92.2 0.0 copy-start.14
  92.2 0.0 copy-start.15
  92.2 1.3 copy-done.14
  93.5 0.6 copy-done.15
  94.0 2.9 convolution_convert_fusion.2
  96.9 4.1 %reshape.111 = bf16[8,16,10,2,320]{4,3,2,1,0:T(2,128)(2,1)S(1)} reshape(bf16[8,320,320]{2,1,0:T(8,128)(2,1)} %convolution_convert_fusion.2) | data formatting | bytes 3276800 | tf_op jit(solution)/shard_map/reshape | solution.py:309
  101.0 2.6 copy.61
  103.6 0.0 copy-start.11
  103.6 0.0 copy-start.13
  103.6 5.1 %reshape.112.tri_ref = bf16[16,5,16,640]{3,2,1,0:T(8,128)(2,1)} reshape(bf16[16,10,8,2,320]{4,3,2,1,0:T(2,128)(2,1)} %bitcast.42) | data formatting | bytes 3276800 | tf_op jit(solution)/shard_map/reshape | solution.py:309
  108.7 0.0 copy-done.11
  108.7 0.0 copy-done.13
  108.7 83.0 %gate_and_back.1 = (bf16[10,640,128]{2,1,0:T(8,128)(2,1)S(1)}, bf16[10,640,128]{2,1,0:T(8,128)(2,1)S(1)}, f32[256,128]{1,0:T(8,128)S(1)}, bf16[16,5,16,640]{3,2,1,0:T(8,128)(2,1)}) custom-call(bf16[16,5,16,640]{3,2,1,0:T(8,128)(2,1)} %reshape.112.tri_ref, bf16[10,640,128]{2,1,0:T(8,128)(2,1)} %copy-done.2, bf16[10,640,128]{2,1,0:T(8,128)(2,1)} %bitcast.48, ...), custom_call_target="tpu_custom_call" | custom-call | tf_op jit(solution)/shard_map/gate_and_back/pallas_call | solution.py:311
  191.7 0.0 copy-start.5
  191.8 1.2 copy-done.5
  192.9 0.0 copy-start.9
  192.9 0.7 copy-done.9
  193.6 5.3 %reshape.115 = bf16[16,10,8,2,320]{4,3,2,1,0:T(2,128)(2,1)} reshape(bf16[16,5,16,640]{3,2,1,0:T(8,128)(2,1)} %get-tuple-element.16) | data formatting | bytes 3276800 | tf_op jit(solution)/shard_map/reshape | solution.py:334
  198.9 4.2 %copy.40 = bf16[8,16,10,2,320]{4,3,2,1,0:T(2,128)(2,1)} copy(bf16[8,16,10,2,320]{4,3,0,2,1:T(2,128)(2,1)} %bitcast.43) | data formatting | bytes 3276800 | tf_op jit(solution)/shard_map/transpose | solution.py:334
  203.0 5.2 %reshape.116 = bf16[8,320,320]{2,1,0:T(8,128)(2,1)} reshape(bf16[8,16,10,2,320]{4,3,2,1,0:T(2,128)(2,1)} %copy.40) | data formatting | bytes 3276800 | tf_op jit(solution)/shard_map/reshape | solution.py:334
  208.3 4.8 %convolution_convert_fusion.1 = bf16[8,320,320]{2,1,0:T(8,128)(2,1)} fusion(bf16[8,320,320]{2,1,0:T(8,128)(2,1)} %reshape.116, bf16[8,320,320]{2,0,1:T(8,128)(2,1)} %bitcast.47), kind=kOutput, calls=%fused_computation.5 | convolution fusion | flops 525107200 | bytes 4915200 | tf_op jit(solution)/shard_map/hkj,hij->hki/dot_general | solution.py:335
  213.0 5.0 %stack.9 = bf16[1,8,16,10,2,320]{5,4,3,2,1,0:T(2,128)(2,1)} reshape(bf16[8,320,320]{2,1,0:T(8,128)(2,1)} %convolution_convert_fusion.1) | data formatting | bytes 3276800 | tf_op jit(solution)/shard_map/stack | solution.py:337
  218.1 4.8 %convolution_convert_fusion = bf16[8,320,320]{2,1,0:T(8,128)(2,1)} fusion(bf16[8,320,320]{2,1,0:T(8,128)(2,1)} %reshape.116, bf16[8,320,320]{2,0,1:T(8,128)(2,1)} %bitcast.45), kind=kOutput, calls=%fused_computation.4 | convolution fusion | flops 525107200 | bytes 4915200 | tf_op jit(solution)/shard_map/hki,hij->hkj/dot_general | solution.py:336
  222.8 5.0 %stack.10 = bf16[1,8,16,10,2,320]{5,4,3,2,1,0:T(2,128)(2,1)} reshape(bf16[8,320,320]{2,1,0:T(8,128)(2,1)} %convolution_convert_fusion) | data formatting | bytes 3276800 | tf_op jit(solution)/shard_map/stack | solution.py:337
  227.9 8.2 %copy_bitcast_fusion = bf16[16,10,2,8,2,320]{5,4,3,2,1,0:T(2,128)(2,1)} fusion(bf16[1,8,16,10,2,320]{5,4,3,2,1,0:T(2,128)(2,1)} %stack.10, bf16[1,8,16,10,2,320]{5,4,3,2,1,0:T(2,128)(2,1)} %stack.9), kind=kLoop, calls=%fused_computation.1 | loop fusion | flops 1638400 | bytes 6553600 | tf_op jit(solution)/shard_map/transpose | solution.py:338
  236.1 0.0 copy-start.1
  236.1 8.9 %reshape.117.dlr_ref = bf16[16,5,32,640]{3,2,1,0:T(8,128)(2,1)} reshape(bf16[16,10,2,8,2,320]{5,4,3,2,1,0:T(2,128)(2,1)} %copy_bitcast_fusion) | data formatting | bytes 6553600 | tf_op jit(solution)/shard_map/reshape | solution.py:338
  245.0 0.1 copy.44.w_ref
  245.1 0.0 copy-done.1
  245.1 0.0 copy-start.8
  245.1 0.7 copy-done.8
  245.9 0.0 copy-start.10
  245.9 0.9 copy-done.10
  246.8 0.0 copy-start.12
  246.8 0.8 copy-done.12
  247.5 98.8 %pair_gradient.1 = (bf16[10,640,128]{2,1,0:T(8,128)(2,1)S(1)}, f32[16,48,128]{2,1,0:T(8,128)S(1)}) custom-call(bf16[16,5,32,640]{3,2,1,0:T(8,128)(2,1)} %reshape.117.dlr_ref, bf16[10,640,128]{2,1,0:T(8,128)(2,1)S(1)} %bitcast.33, bf16[10,640,128]{2,1,0:T(8,128)(2,1)} %copy-done.2, bf16[10,640,128]{2,1,0:T(8,128)(2,1)} %copy-done.5, ...), custom_call_target="tpu_custom_call" | custom-call | tf_op jit(solution)/shard_map/pair_gradient/pallas_call | solution.py:342
  346.3 0.0 copy-start.3
  346.3 1.2 copy-done.3
  347.5 0.0 copy-start.6
  347.5 0.8 copy.45
  348.3 0.0 copy-done.6
  348.3 0.0 copy-start.4
  348.3 1.9 copy.46
  350.2 1.5 fusion.5
  351.8 1.2 copy.64
  352.9 0.0 copy-done.4
  352.9 1.2 copy.65
  (4 shorter events, 0.1 us)
Async XLA Ops:
  1.8 87.2 %copy-start.7 = (f32[10,1,640]{2,1,0:T(1,128)}, f32[10,1,640]{2,1,0:T(1,128)S(1)}, u32[]{:S(2)}) copy-start(f32[10,1,640]{2,1,0:T(1,128)S(1)} %broadcast_multiply_fusion.mask_ref) | copy-start | bytes 76804
  2.9 1.4 copy-start
  78.6 1.2 copy-start.2
  92.2 1.3 copy-start.14
  92.2 1.8 copy-start.15
  103.6 5.1 %copy-start.11 = (bf16[128,128]{1,0:T(8,128)(2,1)S(1)}, bf16[128,128]{1,0:T(8,128)(2,1)}, u32[]{:S(2)}) copy-start(bf16[128,128]{1,0:T(8,128)(2,1)} %w_gate_ref.3) | copy-start | bytes 98308
  103.6 5.1 %copy-start.13 = (bf16[128,128]{1,0:T(8,128)(2,1)S(1)}, bf16[128,128]{1,0:T(8,128)(2,1)}, u32[]{:S(2)}) copy-start(bf16[128,128]{1,0:T(8,128)(2,1)} %w_out_ref.1) | copy-start | bytes 98308
  191.7 1.2 copy-start.5
  192.9 0.7 copy-start.9
  236.1 9.0 %copy-start.1 = (bf16[20,320,128]{2,1,0:T(8,128)(2,1)S(1)}, bf16[20,320,128]{2,1,0:T(8,128)(2,1)}, u32[]{:S(2)}) copy-start(bf16[20,320,128]{2,1,0:T(8,128)(2,1)} %param.6) | copy-start | bytes 4915204
  245.1 0.7 copy-start.8
  245.9 0.9 copy-start.10
  246.8 0.8 copy-start.12
  346.3 1.2 copy-start.3
  347.5 0.8 copy-start.6
  348.3 4.6 %copy-start.4 = (bf16[10,640,128]{2,1,0:T(8,128)(2,1)S(1)}, bf16[10,640,128]{2,1,0:T(8,128)(2,1)}, u32[]{:S(2)}) copy-start(bf16[10,640,128]{2,1,0:T(8,128)(2,1)} %copy-done.3) | copy-start | bytes 4915204

commit v2 on v1

--- a/solution.py
+++ b/solution.py
@@ -12,6 +12,7 @@
 BF16 = jnp.bfloat16
 EPS = 1e-05
 AXIS = "dap"
+LANES = 128
 
 
 def greet(n):
@@ -259,6 +260,81 @@
     loop(chunks, lambda c: await_send(n, c, dlr_ref, recv, in_send_sem, in_recv_sem))
 
 
+def take(ref, start, count, stride):
+    return jnp.concatenate([ref[t, pl.ds(start, count, stride=stride), :] for t in range(ref.shape[0])], axis=1)
+
+
+def put(ref, start, count, stride, values):
+    short = ref.shape[0] * LANES - values.shape[1]
+    if short:
+        values = jnp.concatenate([values, jnp.zeros((values.shape[0], short), values.dtype)], axis=1)
+    for t in range(ref.shape[0]):
+        ref[t, pl.ds(start, count, stride=stride), :] = values[:, t * LANES : (t + 1) * LANES]
+
+
+def unfold(wide, start, stride, fold):
+    block = take(wide, start, wide.shape[1] // stride, stride).astype(BF16)
+    crop = block.shape[1] // fold
+    return jnp.concatenate([block[:, f * crop : (f + 1) * crop] for f in range(fold)], axis=0)
+
+
+def refold(values, fold):
+    count = values.shape[0] // fold
+    return jnp.concatenate([values[f * count : (f + 1) * count, :] for f in range(fold)], axis=1)
+
+
+def widen(n, src, wide):
+    size = src.shape[1] * src.shape[2]
+
+    def one(d):
+        block = src[d].astype(F32).reshape((size, src.shape[3]))
+        for t in range(wide.shape[0]):
+            wide[t, pl.ds(pl.multiple_of(d * size, 8), size), :] = block[:, t * LANES : (t + 1) * LANES]
+
+    loop(n, one)
+
+
+def narrow(n, wide, dst):
+    size = dst.shape[1] * dst.shape[2]
+
+    def one(d):
+        parts = [wide[t, pl.ds(pl.multiple_of(d * size, 8), size), :] for t in range(wide.shape[0])]
+        dst[d] = jnp.concatenate(parts, axis=1).reshape(dst.shape[1:]).astype(BF16)
+
+    loop(n, one)
+
+
+def triangle_kernel(n, hd, fold, lr_ref, tri_ref, sides_ref, wide, rows, wire):
+    widen(n, lr_ref, wide)
+    count = wire.shape[1] // hd
+    crop = sides_ref.shape[3]
+    for h in range(hd):
+        left = unfold(wide, h, 2 * hd, fold)
+        right = unfold(wide, hd + h, 2 * hd, fold)
+        sides_ref[0, h] = left
+        sides_ref[1, h] = right
+        put(rows, 0, count * fold, 1, dot(left, right, 0, 0))
+        parts = [take(rows, f, count, fold)[:, :crop] for f in range(fold)]
+        put(wire, h, count, hd, jnp.concatenate(parts, axis=1))
+    narrow(n, wire, tri_ref)
+
+
+def triangle_back_kernel(n, hd, fold, d_tri_ref, sides_ref, dlr_ref, wide, rows, wire):
+    widen(n, d_tri_ref, wire)
+    count = wire.shape[1] // hd
+    crop = sides_ref.shape[3]
+    for h in range(hd):
+        block = take(wire, h, count, hd)
+        for f in range(fold):
+            put(rows, f, count, fold, block[:, f * crop : (f + 1) * crop])
+        d_tri = take(rows, 0, count * fold, 1)[:, :crop].astype(BF16)
+        d_left = dot(sides_ref[1, h], d_tri, 1, 1)
+        d_right = dot(sides_ref[0, h], d_tri, 1, 0)
+        put(wide, h, count, 2 * hd, refold(d_left, fold))
+        put(wide, hd + h, count, 2 * hd, refold(d_right, fold))
+    narrow(n, wide, dlr_ref)
+
+
 VMEM = pl.BlockSpec(memory_space=pltpu.VMEM)
 ANY = pl.BlockSpec(memory_space=pl.ANY)
 DMA = pltpu.SemaphoreType.DMA
@@ -300,13 +376,27 @@
         compiler_params=params(0),
     )(pair_q, pmask, w_perm_t)
 
-    lr = lr.reshape((n, steps, 2, hd, fold, crop)).transpose((2, 3, 0, 1, 4, 5)).reshape((2, hd, n * row_count, crop))
-    left, right = lr[0], lr[1]
-    tri = jnp.einsum("hki,hkj->hij", left, right, preferred_element_type=F32).astype(BF16)
     group3 = 16 // hd
     chunks3 = steps // group3
     tri_shape = (n, chunks3, group3 * hd, width)
-    tri = tri.reshape((hd, n, steps, fold, crop)).transpose((1, 2, 0, 3, 4)).reshape(tri_shape)
+    crop_rows = n * row_count
+    relayout = [
+        pltpu.VMEM((width // LANES, n * steps * 2 * hd, LANES), F32),
+        pltpu.VMEM(((crop + LANES - 1) // LANES, crop_rows, LANES), F32),
+        pltpu.VMEM((width // LANES, n * steps * hd, LANES), F32),
+    ]
+    tri, sides = pl.pallas_call(
+        functools.partial(triangle_kernel, n, hd, fold),
+        name="triangle",
+        out_shape=(
+            jax.ShapeDtypeStruct(tri_shape, BF16),
+            jax.ShapeDtypeStruct((2, hd, crop_rows, crop), BF16),
+        ),
+        in_specs=[VMEM],
+        out_specs=(VMEM, VMEM),
+        scratch_shapes=relayout,
+        compiler_params=pltpu.CompilerParams(vmem_limit_bytes=50 * 1024 * 1024),
+    )(lr)
 
     update, dgp, grads, d_tri = pl.pallas_call(
         functools.partial(middle_kernel, n, chunks3, group3),
@@ -331,11 +421,15 @@
         compiler_params=params(1),
     )(tri, normed, cotan_q, w_gate, w_out)
 
-    d_tri = d_tri.reshape((n, steps, hd, fold, crop)).transpose((2, 0, 1, 3, 4)).reshape((hd, n * row_count, crop))
-    d_left = jnp.einsum("hkj,hij->hki", right, d_tri, preferred_element_type=F32).astype(BF16)
-    d_right = jnp.einsum("hki,hij->hkj", left, d_tri, preferred_element_type=F32).astype(BF16)
-    dlr = jnp.stack([d_left, d_right]).reshape((2, hd, n, steps, fold, crop))
-    dlr = dlr.transpose((2, 3, 0, 1, 4, 5)).reshape(lr_shape)
+    dlr = pl.pallas_call(
+        functools.partial(triangle_back_kernel, n, hd, fold),
+        name="triangle_back",
+        out_shape=jax.ShapeDtypeStruct(lr_shape, BF16),
+        in_specs=[VMEM, VMEM],
+        out_specs=VMEM,
+        scratch_shapes=relayout,
+        compiler_params=pltpu.CompilerParams(vmem_limit_bytes=50 * 1024 * 1024),
+    )(d_tri, sides)
 
     grad_rows = 4 * hidden + hidden + channels
     part = grad_rows // n

time: 358 us -> 298 us (0.83)
  local copies, waits for them, and re-layouts: 75.8 us -> 16.7 us
  Pallas kernels: 256 us -> 276 us
  matrix products: 12.4 us -> 0 us
  other arithmetic: 8.91 us -> 0.7 us
    reshape x8 -> x0, local copies, waits for them, and re-layouts: 43.2 us -> none  [the longest x2 12 us: shards(): lr.reshape((n, steps, 2, hd, fold, crop)).transpose((2, 3, 0, 1, 4, 5))]
    pallas_call x0 -> x2, Pallas kernels: none -> 19.8 us  [the longest x1 9.92 us: shards(): pl.pallas_call(functools.partial(triangle_kernel, n, hd, fold), name='tri...]
    dot_general x3 -> x0, matrix products: 12.4 us -> none  [the longest x1 4.79 us: shards(): jnp.einsum('hkj,hij->hki', right, d_tri, preferred_element_type=F32)]
    another operation x2 -> x0, local copies, waits for them, and re-layouts: 10.1 us -> none  [shards(): dlr = jnp.stack([d_left, d_right]).reshape((2, hd, n, steps, fold, crop))]
    transpose x1 -> x0, other arithmetic: 8.21 us -> none  [shards(): dlr = dlr.transpose((2, 3, 0, 1, 4, 5)).reshape(lr_shape)]
    transpose x1 -> x0, local copies, waits for them, and re-layouts: 4.16 us -> none  [shards(): d_tri.reshape((n, steps, hd, fold, crop)).transpose((2, 0, 1, 3, 4))]
where the time goes in v2:
time: 298 us; the launch traced here: 294 us
  Pallas kernels  276 us (93%)
  local copies, waits for them, and re-layouts  16.7 us (6%)
    pallas_call x1, Pallas kernels, shards(): pl.pallas_call(functools.partial(last_kernel, n, chunks, group, 1.0 / cro...  98.8 us
    pallas_call x1, Pallas kernels, shards(): pl.pallas_call(functools.partial(middle_kernel, n, chunks3, group3), name...  83 us
    pallas_call x1, Pallas kernels, shards(): pl.pallas_call(functools.partial(first_kernel, n, chunks, group), name='p...  74.3 us
    unnamed x36, local copies, waits for them, and re-layouts  14.6 us
    pallas_call x1, Pallas kernels, shards(): pl.pallas_call(functools.partial(triangle_kernel, n, hd, fold), name='tri...  9.92 us
    pallas_call x1, Pallas kernels, shards(): pl.pallas_call(functools.partial(triangle_back_kernel, n, hd, fold), name...  9.89 us

profile of v2, /device:TPU:0, one launch (start us, length us, event | category | flops | bytes accessed | tf_op | source)
XLA Modules:
  0.0 294.2 jit_solution(1615454047843694453)
XLA Ops:
  0.6 0.7 convert_element_type.3
  1.3 0.1 dynamic_slice.3
  1.4 0.1 mul.32
  1.5 0.1 mul.33
  1.6 0.1 mul.34
  1.7 0.1 mul.36
  1.8 0.0 copy-start.9
  1.8 1.0 copy.19
  2.9 0.0 copy-start
  2.9 1.4 copy-done
  4.3 74.3 %project_and_send.1 = (bf16[10,640,128]{2,1,0:T(8,128)(2,1)S(1)}, bf16[16,5,32,640]{3,2,1,0:T(8,128)(2,1)}) custom-call(bf16[10,640,128]{2,1,0:T(8,128)(2,1)S(1)} %bitcast.15, f32[10,1,640]{2,1,0:T(1,128)S(1)} %broadcast_multiply_fusion.mask_ref, bf16[512,128]{1,0:T(8,128)(2,1)S(1)} %bitcast.17), custom_call_target="tpu_custom_call" | custom-call | tf_op jit(solution)/shard_map/project_and_send/pallas_call | solution.py:366
  78.6 0.0 copy-start.2
  78.7 0.0 copy-start.13
  78.7 0.0 copy-start.15
  78.7 9.9 %triangle.1 = (bf16[16,5,16,640]{3,2,1,0:T(8,128)(2,1)S(1)}, bf16[2,8,320,320]{3,2,1,0:T(8,128)(2,1)}) custom-call(bf16[16,5,32,640]{3,2,1,0:T(8,128)(2,1)} %get-tuple-element.15.lr_ref), custom_call_target="tpu_custom_call" | custom-call | tf_op jit(solution)/shard_map/triangle/pallas_call | solution.py:388
  88.6 0.0 copy-done.9
  88.6 0.0 copy-done.2
  88.6 0.0 copy-start.5
  88.6 1.2 copy-done.5
  89.8 0.0 copy-done.13
  89.8 0.0 copy-done.15
  89.8 83.0 %gate_and_back.1 = (bf16[10,640,128]{2,1,0:T(8,128)(2,1)S(1)}, bf16[10,640,128]{2,1,0:T(8,128)(2,1)S(1)}, f32[256,128]{1,0:T(8,128)S(1)}, bf16[16,5,16,640]{3,2,1,0:T(8,128)(2,1)}) custom-call(bf16[16,5,16,640]{3,2,1,0:T(8,128)(2,1)} %copy-done.5, bf16[10,640,128]{2,1,0:T(8,128)(2,1)} %copy-done.2, bf16[10,640,128]{2,1,0:T(8,128)(2,1)} %bitcast.24, ...), custom_call_target="tpu_custom_call" | custom-call | tf_op jit(solution)/shard_map/gate_and_back/pallas_call | solution.py:401
  172.8 0.0 copy-start.6
  172.8 1.2 copy-done.6
  174.0 0.0 copy-start.11
  174.0 0.0 copy-start.7
  174.0 1.5 copy-done.7
  175.5 0.0 copy-start.1
  175.5 9.9 %triangle_back.1.dlr_ref = bf16[16,5,32,640]{3,2,1,0:T(8,128)(2,1)} custom-call(bf16[16,5,16,640]{3,2,1,0:T(8,128)(2,1)S(1)} %copy-done.7, bf16[2,8,320,320]{3,2,1,0:T(8,128)(2,1)} %get-tuple-element.20.sides_ref), custom_call_target="tpu_custom_call" | custom-call | tf_op jit(solution)/shard_map/triangle_back/pallas_call | solution.py:424
  185.3 0.0 copy-done.11
  185.4 0.1 copy.21.w_ref
  185.5 0.0 copy-done.1
  185.5 0.0 copy-start.10
  185.5 0.7 copy-done.10
  186.2 0.0 copy-start.12
  186.2 0.9 copy-done.12
  187.1 0.0 copy-start.14
  187.1 0.8 copy-done.14
  187.9 98.8 %pair_gradient.1 = (bf16[10,640,128]{2,1,0:T(8,128)(2,1)S(1)}, f32[16,48,128]{2,1,0:T(8,128)S(1)}) custom-call(bf16[16,5,32,640]{3,2,1,0:T(8,128)(2,1)} %triangle_back.1.dlr_ref, bf16[10,640,128]{2,1,0:T(8,128)(2,1)S(1)} %bitcast.16, bf16[10,640,128]{2,1,0:T(8,128)(2,1)} %copy-done.2, bf16[10,640,128]{2,1,0:T(8,128)(2,1)} %copy-done.6, ...), custom_call_target="tpu_custom_call" | custom-call | tf_op jit(solution)/shard_map/pair_gradient/pallas_call | solution.py:436
  286.7 0.0 copy-start.3
  286.7 1.2 copy-done.3
  287.9 0.0 copy-start.8
  287.9 0.7 copy-done.8
  288.7 0.8 copy.23
  289.5 1.5 fusion
  291.0 0.0 copy-start.4
  291.0 1.2 copy.26
  292.2 0.9 copy-done.4
  293.0 1.2 copy.27
  (5 shorter events, 0.1 us)
Async XLA Ops:
  1.8 86.8 %copy-start.9 = (f32[10,1,640]{2,1,0:T(1,128)}, f32[10,1,640]{2,1,0:T(1,128)S(1)}, u32[]{:S(2)}) copy-start(f32[10,1,640]{2,1,0:T(1,128)S(1)} %broadcast_multiply_fusion.mask_ref) | copy-start | bytes 76804
  2.9 1.4 copy-start
  78.6 10.0 %copy-start.2 = (bf16[10,640,128]{2,1,0:T(8,128)(2,1)}, bf16[10,640,128]{2,1,0:T(8,128)(2,1)S(1)}, u32[]{:S(2)}) copy-start(bf16[10,640,128]{2,1,0:T(8,128)(2,1)S(1)} %get-tuple-element.17.normed_ref) | copy-start | bytes 4915204
  78.7 11.1 %copy-start.13 = (bf16[128,128]{1,0:T(8,128)(2,1)S(1)}, bf16[128,128]{1,0:T(8,128)(2,1)}, u32[]{:S(2)}) copy-start(bf16[128,128]{1,0:T(8,128)(2,1)} %w_gate_ref.3) | copy-start | bytes 98308
  78.7 11.1 %copy-start.15 = (bf16[128,128]{1,0:T(8,128)(2,1)S(1)}, bf16[128,128]{1,0:T(8,128)(2,1)}, u32[]{:S(2)}) copy-start(bf16[128,128]{1,0:T(8,128)(2,1)} %w_out_ref.1) | copy-start | bytes 98308
  88.6 1.2 copy-start.5
  172.8 1.2 copy-start.6
  174.0 11.4 %copy-start.11 = (f32[256,128]{1,0:T(8,128)}, f32[256,128]{1,0:T(8,128)S(1)}, u32[]{:S(2)}) copy-start(f32[256,128]{1,0:T(8,128)S(1)} %get-tuple-element.22.grad_ref) | copy-start | bytes 393220
  174.0 1.5 copy-start.7
  175.5 10.0 %copy-start.1 = (bf16[20,320,128]{2,1,0:T(8,128)(2,1)S(1)}, bf16[20,320,128]{2,1,0:T(8,128)(2,1)}, u32[]{:S(2)}) copy-start(bf16[20,320,128]{2,1,0:T(8,128)(2,1)} %param.6) | copy-start | bytes 4915204
  185.5 0.7 copy-start.10
  186.2 0.9 copy-start.12
  187.1 0.8 copy-start.14
  286.7 1.2 copy-start.3
  287.9 0.7 copy-start.8
  291.0 2.0 copy-start.4

commit v3 on v2

--- a/solution.py
+++ b/solution.py
@@ -335,6 +335,211 @@
     narrow(n, wide, dlr_ref)
 
 
+def fused_kernel(
+    n, hd, fold, chunks, group, chunks3, group3, scale,
+    pair_ref, cotan_ref, mask_ref, w_t_ref, w_ref, w_gate_ref, w_out_ref,
+    update_ref, d_pair_ref, total_ref,
+    lr_send, lr_recv, dlr_send, dlr_recv, tri_send, tri_recv, dt_send, dt_recv,
+    wide, rows_f, wire, sides, normed_s, dgp_s, grads, d_proj, sums, slices, gathered,
+    lr_ss, lr_rs, dlr_ss, dlr_rs, tri_ss, tri_rs, dt_ss, dt_rs, rs_send, rs_recv, ag_send, ag_recv,
+):
+    me = lax.axis_index(AXIS)
+    greet(n)
+    full, channels = w_t_ref.shape
+    half = full // 2
+    hidden = w_out_ref.shape[0]
+    lr_rows = 2 * hd
+    width = pair_ref.shape[1]
+    crop = sides.shape[3]
+    part = sums.shape[0] // n
+
+    def spread(block, dst, row, size):
+        values = block.astype(F32)
+        for t in range(dst.shape[0]):
+            dst[t, pl.ds(pl.multiple_of(row, 8), size), :] = values[:, t * LANES : (t + 1) * LANES]
+
+    def collect(c, count, src, dst, own, ss, rs, wide_ref):
+        size = src.shape[2]
+        spread(own[me, c], wide_ref, (me * count + c) * size, size)
+
+        def one(step, carry):
+            peer = lax.rem(me + n - step, n)
+            push(src.at[peer, c], dst.at[peer, c], ss.at[c, peer], rs.at[c, peer], peer).wait_recv()
+            spread(dst[peer, c], wide_ref, (peer * count + c) * size, size)
+            return carry
+
+        lax.fori_loop(1, n, one, 0)
+
+    def distribute(c, count, wide_ref, src, dst, ss, rs):
+        size = src.shape[2]
+
+        def one(d):
+            row = pl.multiple_of((d * count + c) * size, 8)
+            parts = [wide_ref[t, pl.ds(row, size), :] for t in range(wide_ref.shape[0])]
+            src[d, c] = jnp.concatenate(parts, axis=1).astype(BF16)
+
+        loop(n, one)
+        dst[me, c] = src[me, c]
+        push_chunk(n, c, src, dst, ss, rs)
+
+    def project(c):
+        for j in range(group):
+            q = c * group + j
+            x = pair_ref[q].astype(F32)
+            center = x - jnp.mean(x, axis=-1, keepdims=True)
+            inverse = lax.rsqrt(jnp.mean(center * center, axis=-1, keepdims=True) + EPS)
+            normed = (center * inverse).astype(BF16)
+            normed_s[q] = normed
+            lin = dot(w_t_ref[0:half, :], normed, 1, 1)
+            gate = dot(w_t_ref[half:, :], normed, 1, 1)
+            gated = (mask_ref[q] * jax.nn.sigmoid(gate) * lin).reshape((n, lr_rows, width))
+            lr_send[:, c, j * lr_rows : (j + 1) * lr_rows, :] = gated.astype(BF16)
+        push_chunk(n, c, lr_send, lr_recv, lr_ss, lr_rs)
+
+    loop(chunks, project)
+    grads[...] = jnp.zeros_like(grads)
+    loop(chunks, lambda c: collect(c, chunks, lr_send, lr_recv, lr_send, lr_ss, lr_rs, wide))
+
+    count = wire.shape[1] // hd
+    for h in range(hd):
+        left = unfold(wide, h, lr_rows, fold)
+        right = unfold(wide, hd + h, lr_rows, fold)
+        sides[0, h] = left
+        sides[1, h] = right
+        put(rows_f, 0, count * fold, 1, dot(left, right, 0, 0))
+        parts = [take(rows_f, f, count, fold)[:, :crop] for f in range(fold)]
+        put(wire, h, count, hd, jnp.concatenate(parts, axis=1))
+    loop(chunks3, lambda c: distribute(c, chunks3, wire, tri_send, tri_recv, tri_ss, tri_rs))
+
+    def middle(c):
+        await_recv(n, c, tri_send, tri_recv, tri_ss, tri_rs)
+        block = tri_recv[:, c].astype(F32)
+        parts = []
+        for j in range(group3):
+            q = c * group3 + j
+            tri = block[:, j * hd : (j + 1) * hd, :].reshape((hidden, width))
+            center = tri - jnp.mean(tri, axis=0, keepdims=True)
+            inverse = lax.rsqrt(jnp.mean(center * center, axis=0, keepdims=True) + EPS)
+            hat = center * inverse
+            tri_normed = hat.astype(BF16)
+            value = dot(tri_normed, w_out_ref[...], 0, 0)
+            normed = normed_s[q]
+            out_gate = jax.nn.sigmoid(dot(normed, w_gate_ref[...], 1, 0))
+            cotan = cotan_ref[q].astype(F32)
+            update_ref[q] = (out_gate * value).astype(BF16)
+            d_value = (cotan * out_gate).astype(BF16)
+            dgp = (cotan * value * out_gate * (1.0 - out_gate)).astype(BF16)
+            dgp_s[q] = dgp
+            grads[full : full + hidden, :] += dot(tri_normed, d_value, 1, 0)
+            grads[full + hidden :, :] += dot(normed, dgp, 0, 0)
+            d_tn = dot(w_out_ref[...], d_value, 1, 1)
+            shifted = d_tn - jnp.mean(d_tn, axis=0, keepdims=True)
+            d_tri = inverse * (shifted - hat * jnp.mean(d_tn * hat, axis=0, keepdims=True))
+            parts.append(d_tri.reshape((n, hd, width)))
+        dt_send[:, c] = jnp.concatenate(parts, axis=1).astype(BF16)
+        push_chunk(n, c, dt_send, dt_recv, dt_ss, dt_rs)
+
+    loop(chunks3, middle)
+    loop(chunks3, lambda c: collect(c, chunks3, dt_send, dt_recv, dt_send, dt_ss, dt_rs, wire))
+
+    for h in range(hd):
+        block = take(wire, h, count, hd)
+        for f in range(fold):
+            put(rows_f, f, count, fold, block[:, f * crop : (f + 1) * crop])
+        d_tri = take(rows_f, 0, count * fold, 1)[:, :crop].astype(BF16)
+        put(wide, h, count, lr_rows, refold(dot(sides[1, h], d_tri, 1, 1), fold))
+        put(wide, hd + h, count, lr_rows, refold(dot(sides[0, h], d_tri, 1, 0), fold))
+    loop(chunks, lambda c: distribute(c, chunks, wide, dlr_send, dlr_recv, dlr_ss, dlr_rs))
+
+    def back_projection(c):
+        await_recv(n, c, dlr_send, dlr_recv, dlr_ss, dlr_rs)
+        block = dlr_recv[:, c].astype(F32)
+        for j in range(group):
+            q = c * group + j
+            cotan = block[:, j * lr_rows : (j + 1) * lr_rows, :].reshape((half, width)) * mask_ref[q]
+            normed = normed_s[q]
+            lin = dot(w_t_ref[0:half, :], normed, 1, 1)
+            sig = jax.nn.sigmoid(dot(w_t_ref[half:, :], normed, 1, 1))
+            d_lin = cotan * sig
+            d_gate = (d_lin * lin * (1.0 - sig)).astype(BF16)
+            d_lin = d_lin.astype(BF16)
+            grads[0:half, :] += dot(d_lin, normed, 1, 0)
+            grads[half:full, :] += dot(d_gate, normed, 1, 0)
+            d_proj[j, 0:half, :] = d_lin
+            d_proj[j, half:, :] = d_gate
+
+    def pair_gradient(c):
+        for j in range(group):
+            q = c * group + j
+            d_normed = dot(w_ref[...], d_proj[j], 1, 0)
+            d_normed = d_normed.T + dot(dgp_s[q], w_gate_ref[...], 1, 1)
+            x = pair_ref[q].astype(F32)
+            center = x - jnp.mean(x, axis=-1, keepdims=True)
+            inverse = lax.rsqrt(jnp.mean(center * center, axis=-1, keepdims=True) + EPS)
+            hat = center * inverse
+            shifted = d_normed - jnp.mean(d_normed, axis=-1, keepdims=True)
+            d_pair = inverse * (shifted - hat * jnp.mean(d_normed * hat, axis=-1, keepdims=True))
+            d_pair_ref[q] = d_pair.astype(BF16)
+
+    def both(c):
+        back_projection(c)
+        pair_gradient(c)
+
+    loop(chunks - 1, both)
+    back_projection(chunks - 1)
+    sums[...] = grads[...].astype(BF16)
+
+    def own_rows(d):
+        return sums.at[pl.ds(pl.multiple_of(d * part, 16), part), :]
+
+    def scatter(step, carry):
+        peer = lax.rem(me + step, n)
+        push(own_rows(peer), slices.at[me], rs_send.at[peer], rs_recv.at[me], peer).start()
+        return carry
+
+    lax.fori_loop(1, n, scatter, 0)
+    slices[me] = sums[pl.ds(pl.multiple_of(me * part, 16), part), :]
+    pair_gradient(chunks - 1)
+
+    def scattered(step, carry):
+        peer = lax.rem(me + n - step, n)
+        push(own_rows(peer), slices.at[peer], rs_send.at[peer], rs_recv.at[peer], peer).wait_recv()
+        return carry
+
+    lax.fori_loop(1, n, scattered, 0)
+    total = slices[0].astype(F32)
+    for d in range(1, n):
+        total = total + slices[d].astype(F32)
+    gathered[me] = (total * scale).astype(BF16)
+
+    def gather(step, carry):
+        peer = lax.rem(me + step, n)
+        push(gathered.at[me], gathered.at[me], ag_send.at[peer], ag_recv.at[me], peer).start()
+        return carry
+
+    lax.fori_loop(1, n, gather, 0)
+    loop(chunks, lambda c: await_send(n, c, lr_send, lr_recv, lr_ss, lr_rs))
+    loop(chunks3, lambda c: await_send(n, c, tri_send, tri_recv, tri_ss, tri_rs))
+    loop(chunks3, lambda c: await_send(n, c, dt_send, dt_recv, dt_ss, dt_rs))
+    loop(chunks, lambda c: await_send(n, c, dlr_send, dlr_recv, dlr_ss, dlr_rs))
+
+    def arrived(step, carry):
+        peer = lax.rem(me + n - step, n)
+        push(gathered.at[me], gathered.at[peer], ag_send.at[peer], ag_recv.at[peer], peer).wait_recv()
+        return carry
+
+    lax.fori_loop(1, n, arrived, 0)
+
+    def sent(step, carry):
+        peer = lax.rem(me + step, n)
+        push(own_rows(peer), slices.at[me], rs_send.at[peer], rs_recv.at[me], peer).wait_send()
+        push(gathered.at[me], gathered.at[me], ag_send.at[peer], ag_recv.at[me], peer).wait_send()
+        return carry
+
+    lax.fori_loop(1, n, sent, 0)
+    total_ref[...] = gathered[...].astype(F32)
+
+
 VMEM = pl.BlockSpec(memory_space=pltpu.VMEM)
 ANY = pl.BlockSpec(memory_space=pl.ANY)
 DMA = pltpu.SemaphoreType.DMA
@@ -363,19 +568,6 @@
     group = 32 // (2 * hd)
     chunks = steps // group
     lr_shape = (n, chunks, group * 2 * hd, width)
-    normed, lr = pl.pallas_call(
-        functools.partial(first_kernel, n, chunks, group),
-        name="project_and_send",
-        out_shape=(
-            jax.ShapeDtypeStruct((steps, width, channels), BF16),
-            jax.ShapeDtypeStruct(lr_shape, BF16),
-        ),
-        in_specs=[VMEM] * 3,
-        out_specs=(VMEM, ANY),
-        scratch_shapes=[pltpu.VMEM(lr_shape, BF16), DMA((chunks, n)), DMA((chunks, n)), DMA],
-        compiler_params=params(0),
-    )(pair_q, pmask, w_perm_t)
-
     group3 = 16 // hd
     chunks3 = steps // group3
     tri_shape = (n, chunks3, group3 * hd, width)
@@ -385,77 +577,123 @@
         pltpu.VMEM(((crop + LANES - 1) // LANES, crop_rows, LANES), F32),
         pltpu.VMEM((width // LANES, n * steps * hd, LANES), F32),
     ]
-    tri, sides = pl.pallas_call(
-        functools.partial(triangle_kernel, n, hd, fold),
-        name="triangle",
-        out_shape=(
-            jax.ShapeDtypeStruct(tri_shape, BF16),
-            jax.ShapeDtypeStruct((2, hd, crop_rows, crop), BF16),
-        ),
-        in_specs=[VMEM],
-        out_specs=(VMEM, VMEM),
-        scratch_shapes=relayout,
-        compiler_params=pltpu.CompilerParams(vmem_limit_bytes=50 * 1024 * 1024),
-    )(lr)
-
-    update, dgp, grads, d_tri = pl.pallas_call(
-        functools.partial(middle_kernel, n, chunks3, group3),
-        name="gate_and_back",
-        out_shape=(
-            jax.ShapeDtypeStruct((steps, width, channels), BF16),
-            jax.ShapeDtypeStruct((steps, width, channels), BF16),
-            jax.ShapeDtypeStruct((hidden + channels, channels), F32),
-            jax.ShapeDtypeStruct(tri_shape, BF16),
-        ),
-        in_specs=[ANY] + [VMEM] * 4,
-        out_specs=(VMEM, VMEM, VMEM, ANY),
-        scratch_shapes=[
-            pltpu.VMEM(tri_shape, BF16),
-            pltpu.VMEM(tri_shape, BF16),
-            DMA((chunks3, n)),
-            DMA((chunks3, n)),
-            DMA((chunks3, n)),
-            DMA((chunks3, n)),
-            DMA((2,)),
-        ],
-        compiler_params=params(1),
-    )(tri, normed, cotan_q, w_gate, w_out)
-
-    dlr = pl.pallas_call(
-        functools.partial(triangle_back_kernel, n, hd, fold),
-        name="triangle_back",
-        out_shape=jax.ShapeDtypeStruct(lr_shape, BF16),
-        in_specs=[VMEM, VMEM],
-        out_specs=VMEM,
-        scratch_shapes=relayout,
-        compiler_params=pltpu.CompilerParams(vmem_limit_bytes=50 * 1024 * 1024),
-    )(d_tri, sides)
-
     grad_rows = 4 * hidden + hidden + channels
     part = grad_rows // n
-    d_pair, total = pl.pallas_call(
-        functools.partial(last_kernel, n, chunks, group, 1.0 / crop),
-        name="pair_gradient",
-        out_shape=(
-            jax.ShapeDtypeStruct((steps, width, channels), BF16),
-            jax.ShapeDtypeStruct((n, part, channels), F32),
-        ),
-        in_specs=[ANY] + [VMEM] * 8,
-        out_specs=(VMEM, VMEM),
-        scratch_shapes=[
-            pltpu.VMEM(lr_shape, BF16),
+    if part % 16 == 0 and 54 * pair.size < 48 * 1024 * 1024:
+        buffers = [lr_shape] * 4 + [tri_shape] * 4
+        rest = [
+            pltpu.VMEM((2, hd, crop_rows, crop), BF16),
+            pltpu.VMEM((steps, width, channels), BF16),
+            pltpu.VMEM((steps, width, channels), BF16),
             pltpu.VMEM((grad_rows, channels), F32),
-            pltpu.VMEM((n, part, channels), F32),
-            DMA((chunks, n)),
-            DMA((chunks, n)),
-            DMA((n,)),
-            DMA((n,)),
-            DMA((n,)),
-            DMA((n,)),
-            DMA,
-        ],
-        compiler_params=params(2),
-    )(dlr, pair_q, normed, dgp, pmask, w_perm_t, w_perm, w_gate, grads)
+            pltpu.VMEM((group, 4 * hidden, width), BF16),
+            pltpu.VMEM((grad_rows, channels), BF16),
+            pltpu.VMEM((n, part, channels), BF16),
+            pltpu.VMEM((n, part, channels), BF16),
+        ]
+        update, d_pair, total = pl.pallas_call(
+            functools.partial(fused_kernel, n, hd, fold, chunks, group, chunks3, group3, 1.0 / crop),
+            name="triangle_update",
+            out_shape=(
+                jax.ShapeDtypeStruct((steps, width, channels), BF16),
+                jax.ShapeDtypeStruct((steps, width, channels), BF16),
+                jax.ShapeDtypeStruct((n, part, channels), F32),
+            ),
+            in_specs=[VMEM] * 7,
+            out_specs=(VMEM, VMEM, VMEM),
+            scratch_shapes=[pltpu.VMEM(shape, BF16) for shape in buffers]
+            + relayout
+            + rest
+            + [DMA((chunks, n))] * 4
+            + [DMA((chunks3, n))] * 4
+            + [DMA((n,))] * 4,
+            compiler_params=pltpu.CompilerParams(
+                collective_id=3, has_side_effects=True, vmem_limit_bytes=54 * 1024 * 1024
+            ),
+        )(pair_q, cotan_q, pmask, w_perm_t, w_perm, w_gate, w_out)
+    else:
+        normed, lr = pl.pallas_call(
+            functools.partial(first_kernel, n, chunks, group),
+            name="project_and_send",
+            out_shape=(
+                jax.ShapeDtypeStruct((steps, width, channels), BF16),
+                jax.ShapeDtypeStruct(lr_shape, BF16),
+            ),
+            in_specs=[VMEM] * 3,
+            out_specs=(VMEM, ANY),
+            scratch_shapes=[pltpu.VMEM(lr_shape, BF16), DMA((chunks, n)), DMA((chunks, n)), DMA],
+            compiler_params=params(0),
+        )(pair_q, pmask, w_perm_t)
+
+        tri, sides = pl.pallas_call(
+            functools.partial(triangle_kernel, n, hd, fold),
+            name="triangle",
+            out_shape=(
+                jax.ShapeDtypeStruct(tri_shape, BF16),
+                jax.ShapeDtypeStruct((2, hd, crop_rows, crop), BF16),
+            ),
+            in_specs=[VMEM],
+            out_specs=(VMEM, VMEM),
+            scratch_shapes=relayout,
+            compiler_params=pltpu.CompilerParams(vmem_limit_bytes=50 * 1024 * 1024),
+        )(lr)
+
+        update, dgp, grads, d_tri = pl.pallas_call(
+            functools.partial(middle_kernel, n, chunks3, group3),
+            name="gate_and_back",
+            out_shape=(
+                jax.ShapeDtypeStruct((steps, width, channels), BF16),
+                jax.ShapeDtypeStruct((steps, width, channels), BF16),
+                jax.ShapeDtypeStruct((hidden + channels, channels), F32),
+                jax.ShapeDtypeStruct(tri_shape, BF16),
+            ),
+            in_specs=[ANY] + [VMEM] * 4,
+            out_specs=(VMEM, VMEM, VMEM, ANY),
+            scratch_shapes=[
+                pltpu.VMEM(tri_shape, BF16),
+                pltpu.VMEM(tri_shape, BF16),
+                DMA((chunks3, n)),
+                DMA((chunks3, n)),
+                DMA((chunks3, n)),
+                DMA((chunks3, n)),
+                DMA((2,)),
+            ],
+            compiler_params=params(1),
+        )(tri, normed, cotan_q, w_gate, w_out)
+
+        dlr = pl.pallas_call(
+            functools.partial(triangle_back_kernel, n, hd, fold),
+            name="triangle_back",
+            out_shape=jax.ShapeDtypeStruct(lr_shape, BF16),
+            in_specs=[VMEM, VMEM],
+            out_specs=VMEM,
+            scratch_shapes=relayout,
+            compiler_params=pltpu.CompilerParams(vmem_limit_bytes=50 * 1024 * 1024),
+        )(d_tri, sides)
+
+        d_pair, total = pl.pallas_call(
+            functools.partial(last_kernel, n, chunks, group, 1.0 / crop),
+            name="pair_gradient",
+            out_shape=(
+                jax.ShapeDtypeStruct((steps, width, channels), BF16),
+                jax.ShapeDtypeStruct((n, part, channels), F32),
+            ),
+            in_specs=[ANY] + [VMEM] * 8,
+            out_specs=(VMEM, VMEM),
+            scratch_shapes=[
+                pltpu.VMEM(lr_shape, BF16),
+                pltpu.VMEM((grad_rows, channels), F32),
+                pltpu.VMEM((n, part, channels), F32),
+                DMA((chunks, n)),
+                DMA((chunks, n)),
+                DMA((n,)),
+                DMA((n,)),
+                DMA((n,)),
+                DMA((n,)),
+                DMA,
+            ],
+            compiler_params=params(2),
+        )(dlr, pair_q, normed, dgp, pmask, w_perm_t, w_perm, w_gate, grads)
 
     total = total.reshape((grad_rows, channels))
     total_in = total[: 4 * hidden].reshape((2, n, 2, hd, channels)).transpose((4, 2, 0, 1, 3))

time: 298 us -> 264 us (0.89); the launches traced: 294 us -> 264 us
  Pallas kernels: 276 us -> 253 us
  local copies, waits for them, and re-layouts: 16.7 us -> 8.91 us
    pallas_call x5 -> x1, Pallas kernels: 276 us -> 253 us  [shards(): pl.pallas_call(functools.partial(fused_kernel, n, hd, fold, chunks, group...]
    unnamed x36 -> x10, local copies, waits for them, and re-layouts: 14.6 us -> 5.05 us
where the time goes in v3:
time: 264 us
  Pallas kernels  253 us (96%)
  local copies, waits for them, and re-layouts  8.91 us (3%)
    pallas_call x1, Pallas kernels, shards(): pl.pallas_call(functools.partial(fused_kernel, n, hd, fold, chunks, group...  253 us

profile of v3, /device:TPU:0, one launch (start us, length us, event | category | flops | bytes accessed | tf_op | source)
XLA Modules:
  0.0 264.2 jit_solution(13377803014382903022)
XLA Ops:
  0.6 0.7 convert_element_type.3
  1.3 0.1 dynamic_slice.3
  1.4 0.1 mul.36
  1.5 0.1 mul.32
  1.6 0.1 mul.33
  1.6 0.1 mul.34
  1.8 0.6 broadcast_multiply_fusion.mask_ref
  2.4 1.0 copy.18
  3.4 0.0 copy-start.2
  3.5 0.8 copy.20.w_ref
  4.2 0.0 copy-done.2
  4.2 253.2 %triangle_update.1 = (bf16[10,640,128]{2,1,0:T(8,128)(2,1)}, bf16[10,640,128]{2,1,0:T(8,128)(2,1)}, f32[16,48,128]{2,1,0:T(8,128)}) custom-call(bf16[10,640,128]{2,1,0:T(8,128)(2,1)} %bitcast.17, bf16[10,640,128]{2,1,0:T(8,128)(2,1)} %bitcast.18, f32[10,1,640]{2,1,0:T(1,128)} %broadcast_multiply_fusion.mask_ref, bf16[512,128]{1,0:T(8,128)(2,1)} %bitcast.20, ...), custom_call_target="tpu_custom_call" | custom-call | tf_op jit(solution)/shard_map/triangle_update/pallas_call | solution.py:594
  257.5 0.0 copy-start.1
  257.5 1.6 fusion
  259.1 1.0 slice.12
  260.1 0.8 copy.22
  261.0 0.0 copy-done.1
  261.0 0.0 copy-start
  261.0 1.2 copy.25
  262.1 0.9 copy-done
  263.0 1.2 copy.26
  (3 shorter events, 0.0 us)
Async XLA Ops:
  3.4 0.8 copy-start.2
  257.5 3.5 %copy-start.1 = (bf16[10,640,128]{2,1,0:T(8,128)(2,1)S(1)}, bf16[10,640,128]{2,1,0:T(8,128)(2,1)}, u32[]{:S(2)}) copy-start(bf16[10,640,128]{2,1,0:T(8,128)(2,1)} %get-tuple-element.8) | copy-start | bytes 4915204
  261.0 2.0 copy-start

commit v4 on v3

--- a/solution.py
+++ b/solution.py
@@ -336,7 +336,7 @@
 
 
 def fused_kernel(
-    n, hd, fold, chunks, group, chunks3, group3, scale,
+    n, hd, fold, splits, chunks, group, chunks3, group3, scale,
     pair_ref, cotan_ref, mask_ref, w_t_ref, w_ref, w_gate_ref, w_out_ref,
     update_ref, d_pair_ref, total_ref,
     lr_send, lr_recv, dlr_send, dlr_recv, tri_send, tri_recv, dt_send, dt_recv,
@@ -348,7 +348,8 @@
     full, channels = w_t_ref.shape
     half = full // 2
     hidden = w_out_ref.shape[0]
-    lr_rows = 2 * hd
+    lr_rows = 2 * hd // splits
+    span = hd // splits
     width = pair_ref.shape[1]
     crop = sides.shape[3]
     part = sums.shape[0] // n
@@ -358,29 +359,33 @@
         for t in range(dst.shape[0]):
             dst[t, pl.ds(pl.multiple_of(row, 8), size), :] = values[:, t * LANES : (t + 1) * LANES]
 
-    def collect(c, count, src, dst, own, ss, rs, wide_ref):
+    def collect(c, s, count, src, dst, own, ss, rs, wide_ref):
         size = src.shape[2]
-        spread(own[me, c], wide_ref, (me * count + c) * size, size)
+        base = s * n * count * size
+        i = s * count + c
+        spread(own[me, i], wide_ref, base + (me * count + c) * size, size)
 
         def one(step, carry):
             peer = lax.rem(me + n - step, n)
-            push(src.at[peer, c], dst.at[peer, c], ss.at[c, peer], rs.at[c, peer], peer).wait_recv()
-            spread(dst[peer, c], wide_ref, (peer * count + c) * size, size)
+            push(src.at[peer, i], dst.at[peer, i], ss.at[i, peer], rs.at[i, peer], peer).wait_recv()
+            spread(dst[peer, i], wide_ref, base + (peer * count + c) * size, size)
             return carry
 
         lax.fori_loop(1, n, one, 0)
 
-    def distribute(c, count, wide_ref, src, dst, ss, rs):
+    def distribute(c, s, count, wide_ref, src, dst, ss, rs):
         size = src.shape[2]
+        base = s * n * count * size
+        i = s * count + c
 
         def one(d):
-            row = pl.multiple_of((d * count + c) * size, 8)
+            row = pl.multiple_of(base + (d * count + c) * size, 8)
             parts = [wide_ref[t, pl.ds(row, size), :] for t in range(wide_ref.shape[0])]
-            src[d, c] = jnp.concatenate(parts, axis=1).astype(BF16)
+            src[d, i] = jnp.concatenate(parts, axis=1).astype(BF16)
 
         loop(n, one)
-        dst[me, c] = src[me, c]
-        push_chunk(n, c, src, dst, ss, rs)
+        dst[me, i] = src[me, i]
+        push_chunk(n, i, src, dst, ss, rs)
 
     def project(c):
         for j in range(group):
@@ -392,24 +397,34 @@
             normed_s[q] = normed
             lin = dot(w_t_ref[0:half, :], normed, 1, 1)
             gate = dot(w_t_ref[half:, :], normed, 1, 1)
-            gated = (mask_ref[q] * jax.nn.sigmoid(gate) * lin).reshape((n, lr_rows, width))
-            lr_send[:, c, j * lr_rows : (j + 1) * lr_rows, :] = gated.astype(BF16)
+            gated = (mask_ref[q] * jax.nn.sigmoid(gate) * lin).reshape((n, splits, lr_rows, width))
+            for s in range(splits):
+                lr_send[:, s * chunks + c, j * lr_rows : (j + 1) * lr_rows, :] = gated[:, s].astype(BF16)
         push_chunk(n, c, lr_send, lr_recv, lr_ss, lr_rs)
 
     loop(chunks, project)
+    for s in range(1, splits):
+        loop(chunks, lambda c: push_chunk(n, s * chunks + c, lr_send, lr_recv, lr_ss, lr_rs))
     grads[...] = jnp.zeros_like(grads)
-    loop(chunks, lambda c: collect(c, chunks, lr_send, lr_recv, lr_send, lr_ss, lr_rs, wide))
 
     count = wire.shape[1] // hd
-    for h in range(hd):
-        left = unfold(wide, h, lr_rows, fold)
-        right = unfold(wide, hd + h, lr_rows, fold)
-        sides[0, h] = left
-        sides[1, h] = right
-        put(rows_f, 0, count * fold, 1, dot(left, right, 0, 0))
-        parts = [take(rows_f, f, count, fold)[:, :crop] for f in range(fold)]
-        put(wire, h, count, hd, jnp.concatenate(parts, axis=1))
-    loop(chunks3, lambda c: distribute(c, chunks3, wire, tri_send, tri_recv, tri_ss, tri_rs))
+
+    def side(s, t, k):
+        block = take(wide, s * count * lr_rows + t * span + k, count, lr_rows).astype(BF16)
+        return jnp.concatenate([block[:, f * crop : (f + 1) * crop] for f in range(fold)], axis=0)
+
+    for s in range(splits):
+        loop(chunks, lambda c: collect(c, s, chunks, lr_send, lr_recv, lr_send, lr_ss, lr_rs, wide))
+        for k in range(span):
+            h = s * span + k
+            left = side(s, 0, k)
+            right = side(s, 1, k)
+            sides[0, h] = left
+            sides[1, h] = right
+            put(rows_f, 0, count * fold, 1, dot(left, right, 0, 0))
+            parts = [take(rows_f, f, count, fold)[:, :crop] for f in range(fold)]
+            put(wire, h, count, hd, jnp.concatenate(parts, axis=1))
+    loop(chunks3, lambda c: distribute(c, 0, chunks3, wire, tri_send, tri_recv, tri_ss, tri_rs))
 
     def middle(c):
         await_recv(n, c, tri_send, tri_recv, tri_ss, tri_rs)
@@ -440,23 +455,29 @@
         push_chunk(n, c, dt_send, dt_recv, dt_ss, dt_rs)
 
     loop(chunks3, middle)
-    loop(chunks3, lambda c: collect(c, chunks3, dt_send, dt_recv, dt_send, dt_ss, dt_rs, wire))
-
-    for h in range(hd):
-        block = take(wire, h, count, hd)
-        for f in range(fold):
-            put(rows_f, f, count, fold, block[:, f * crop : (f + 1) * crop])
-        d_tri = take(rows_f, 0, count * fold, 1)[:, :crop].astype(BF16)
-        put(wide, h, count, lr_rows, refold(dot(sides[1, h], d_tri, 1, 1), fold))
-        put(wide, hd + h, count, lr_rows, refold(dot(sides[0, h], d_tri, 1, 0), fold))
-    loop(chunks, lambda c: distribute(c, chunks, wide, dlr_send, dlr_recv, dlr_ss, dlr_rs))
+    loop(chunks3, lambda c: collect(c, 0, chunks3, dt_send, dt_recv, dt_send, dt_ss, dt_rs, wire))
+
+    for s in range(splits):
+        for k in range(span):
+            h = s * span + k
+            block = take(wire, h, count, hd)
+            for f in range(fold):
+                put(rows_f, f, count, fold, block[:, f * crop : (f + 1) * crop])
+            d_tri = take(rows_f, 0, count * fold, 1)[:, :crop].astype(BF16)
+            start = s * count * lr_rows + k
+            put(wide, start, count, lr_rows, refold(dot(sides[1, h], d_tri, 1, 1), fold))
+            put(wide, start + span, count, lr_rows, refold(dot(sides[0, h], d_tri, 1, 0), fold))
+        loop(chunks, lambda c: distribute(c, s, chunks, wide, dlr_send, dlr_recv, dlr_ss, dlr_rs))
 
     def back_projection(c):
-        await_recv(n, c, dlr_send, dlr_recv, dlr_ss, dlr_rs)
-        block = dlr_recv[:, c].astype(F32)
+        blocks = []
+        for s in range(splits):
+            await_recv(n, s * chunks + c, dlr_send, dlr_recv, dlr_ss, dlr_rs)
+            blocks.append(dlr_recv[:, s * chunks + c].astype(F32))
         for j in range(group):
             q = c * group + j
-            cotan = block[:, j * lr_rows : (j + 1) * lr_rows, :].reshape((half, width)) * mask_ref[q]
+            shares = [block[:, j * lr_rows : (j + 1) * lr_rows, :] for block in blocks]
+            cotan = jnp.concatenate(shares, axis=1).reshape((half, width)) * mask_ref[q]
             normed = normed_s[q]
             lin = dot(w_t_ref[0:half, :], normed, 1, 1)
             sig = jax.nn.sigmoid(dot(w_t_ref[half:, :], normed, 1, 1))
@@ -518,10 +539,10 @@
         return carry
 
     lax.fori_loop(1, n, gather, 0)
-    loop(chunks, lambda c: await_send(n, c, lr_send, lr_recv, lr_ss, lr_rs))
+    loop(splits * chunks, lambda c: await_send(n, c, lr_send, lr_recv, lr_ss, lr_rs))
     loop(chunks3, lambda c: await_send(n, c, tri_send, tri_recv, tri_ss, tri_rs))
     loop(chunks3, lambda c: await_send(n, c, dt_send, dt_recv, dt_ss, dt_rs))
-    loop(chunks, lambda c: await_send(n, c, dlr_send, dlr_recv, dlr_ss, dlr_rs))
+    loop(splits * chunks, lambda c: await_send(n, c, dlr_send, dlr_recv, dlr_ss, dlr_rs))
 
     def arrived(step, carry):
         peer = lax.rem(me + n - step, n)
@@ -560,7 +581,10 @@
     mask_all = residue_mask.astype(F32)
     mask_rows = lax.dynamic_slice_in_dim(mask_all, me * row_count, row_count, 0)
     pmask = (mask_rows[:, None] * mask_all[None, :]).reshape((steps, 1, width))
-    w_perm = w_in.reshape((channels, 2, 2, n, hd)).transpose((0, 2, 3, 1, 4)).reshape((channels, 4 * hidden))
+    fused = 6 * hidden % (16 * n) == 0 and 54 * pair.size < 48 * 1024 * 1024
+    splits = 2 if fused and hd % 8 == 0 else 1
+    w_perm = w_in.reshape((channels, 2, 2, n, splits, hd // splits)).transpose((0, 2, 3, 4, 1, 5))
+    w_perm = w_perm.reshape((channels, 4 * hidden))
     w_perm_t = w_perm.T
     pair_q = pair.reshape((steps, width, channels))
     cotan_q = d_out.reshape((steps, width, channels))
@@ -579,8 +603,8 @@
     ]
     grad_rows = 4 * hidden + hidden + channels
     part = grad_rows // n
-    if part % 16 == 0 and 54 * pair.size < 48 * 1024 * 1024:
-        buffers = [lr_shape] * 4 + [tri_shape] * 4
+    if fused:
+        buffers = [(n, splits * chunks, group * 2 * hd // splits, width)] * 4 + [tri_shape] * 4
         rest = [
             pltpu.VMEM((2, hd, crop_rows, crop), BF16),
             pltpu.VMEM((steps, width, channels), BF16),
@@ -592,7 +616,7 @@
             pltpu.VMEM((n, part, channels), BF16),
         ]
         update, d_pair, total = pl.pallas_call(
-            functools.partial(fused_kernel, n, hd, fold, chunks, group, chunks3, group3, 1.0 / crop),
+            functools.partial(fused_kernel, n, hd, fold, splits, chunks, group, chunks3, group3, 1.0 / crop),
             name="triangle_update",
             out_shape=(
                 jax.ShapeDtypeStruct((steps, width, channels), BF16),
@@ -604,7 +628,7 @@
             scratch_shapes=[pltpu.VMEM(shape, BF16) for shape in buffers]
             + relayout
             + rest
-            + [DMA((chunks, n))] * 4
+            + [DMA((splits * chunks, n))] * 4
             + [DMA((chunks3, n))] * 4
             + [DMA((n,))] * 4,
             compiler_params=pltpu.CompilerParams(
@@ -696,7 +720,7 @@
         )(dlr, pair_q, normed, dgp, pmask, w_perm_t, w_perm, w_gate, grads)
 
     total = total.reshape((grad_rows, channels))
-    total_in = total[: 4 * hidden].reshape((2, n, 2, hd, channels)).transpose((4, 2, 0, 1, 3))
+    total_in = total[: 4 * hidden].reshape((2, n, splits, 2, hd // splits, channels)).transpose((5, 3, 0, 1, 2, 4))
     total_in = total_in.reshape((channels, 4 * hidden))
     return (
         update.reshape(pair.shape),

time: 264 us -> 262 us (level)
  no operation moved by 1% of the time
where the time goes in v4:
time: 262 us
  Pallas kernels  251 us (96%)
  local copies, waits for them, and re-layouts  8.96 us (3%)
    pallas_call x1, Pallas kernels, shards(): pl.pallas_call(functools.partial(fused_kernel, n, hd, fold, splits, chunk...  251 us

profile of v4, /device:TPU:0, one launch (start us, length us, event | category | flops | bytes accessed | tf_op | source)
XLA Modules:
  0.0 261.6 jit_solution(15228510397631258618)
XLA Ops:
  0.6 0.7 convert_element_type.3
  1.3 0.1 dynamic_slice.3
  1.4 0.1 mul.36
  1.5 0.1 mul.32
  1.6 0.1 mul.33
  1.6 0.1 mul.34
  1.8 0.6 broadcast_multiply_fusion.mask_ref
  2.4 1.0 copy.14
  3.5 0.0 copy-start.2
  3.5 0.8 copy.16.w_ref
  4.3 0.0 copy-done.2
  4.3 250.6 %triangle_update.1 = (bf16[10,640,128]{2,1,0:T(8,128)(2,1)}, bf16[10,640,128]{2,1,0:T(8,128)(2,1)}, f32[16,48,128]{2,1,0:T(8,128)}) custom-call(bf16[10,640,128]{2,1,0:T(8,128)(2,1)} %bitcast.17, bf16[10,640,128]{2,1,0:T(8,128)(2,1)} %bitcast.18, f32[10,1,640]{2,1,0:T(1,128)} %broadcast_multiply_fusion.mask_ref, bf16[512,128]{1,0:T(8,128)(2,1)} %bitcast.20, ...), custom_call_target="tpu_custom_call" | custom-call | tf_op jit(solution)/shard_map/triangle_update/pallas_call | solution.py:618
  254.9 0.0 copy-start.1
  254.9 1.6 fusion
  256.5 1.0 slice.12
  257.6 0.8 copy.18
  258.4 0.0 copy-done.1
  258.4 0.0 copy-start
  258.4 1.2 copy.21
  259.6 0.9 copy-done
  260.4 1.2 copy.22
  (3 shorter events, 0.1 us)
Async XLA Ops:
  3.5 0.8 copy-start.2
  254.9 3.5 %copy-start.1 = (bf16[10,640,128]{2,1,0:T(8,128)(2,1)S(1)}, bf16[10,640,128]{2,1,0:T(8,128)(2,1)}, u32[]{:S(2)}) copy-start(bf16[10,640,128]{2,1,0:T(8,128)(2,1)} %get-tuple-element.8) | copy-start | bytes 4915204
  258.4 2.0 copy-start
